TPU v7x, 32 devices: a whole 2x2x4 slice. The times are simulated.
32 devices in a mesh: fsdp: 16 (over z, x, core), rep: 2 (over y).
Axes of the slice: x: 2, y: 2, z: 4, core: 2. Of those that a mesh axis runs over, the one named last changes fastest.
Arguments:
- tokens: bfloat16 [1024, 64, 768], P(('fsdp', 'rep')), may hold values from -6 to 6
- counts: int32 [1024], P(('fsdp', 'rep')), may hold values from 40 to 60, as said below
- cotangent: bfloat16 [1024, 64, 768], P(('fsdp', 'rep')), may hold values from -6 to 6
- first_gain: bfloat16 [768], P('fsdp'), may hold values from 0.25 to 1.75
- first_shift: bfloat16 [768], P('fsdp'), may hold values from -1.75 to 1.75
- in_proj: bfloat16 [768, 2304], P('fsdp'), may hold values from -0.21875 to 0.21875
- query_bias: bfloat16 [768], P('fsdp'), may hold values from -3 to 3
- value_bias: bfloat16 [768], P('fsdp'), may hold values from -3 to 3
- out_proj: bfloat16 [768, 768], P('fsdp'), may hold values from -0.875 to 0.875
- out_bias: bfloat16 [768], P('fsdp'), may hold values from -1.75 to 1.75
- second_gain: bfloat16 [768], P('fsdp'), may hold values from 0.25 to 1.75
- second_shift: bfloat16 [768], P('fsdp'), may hold values from -1.75 to 1.75
- up_proj: bfloat16 [768, 3072], P('fsdp'), may hold values from -0.21875 to 0.21875
- hidden_bias: bfloat16 [3072], P('fsdp'), may hold values from -3 to 3
- down_proj: bfloat16 [3072, 768], P('fsdp'), may hold values from -0.15625 to 0.15625
- down_bias: bfloat16 [768], P('fsdp'), may hold values from -1.75 to 1.75
Outputs:
- mixed: bfloat16 [1024, 64, 768], P(('fsdp', 'rep'))
- tokens_grad: bfloat16 [1024, 64, 768], P(('fsdp', 'rep'))
- first_gain_grad: float32 [768], P('fsdp')
- first_shift_grad: float32 [768], P('fsdp')
- in_proj_grad: float32 [768, 2304], P('fsdp')
- query_bias_grad: float32 [768], P('fsdp')
- value_bias_grad: float32 [768], P('fsdp')
- out_proj_grad: float32 [768, 768], P('fsdp')
- out_bias_grad: float32 [768], P('fsdp')
- second_gain_grad: float32 [768], P('fsdp')
- second_shift_grad: float32 [768], P('fsdp')
- up_proj_grad: float32 [768, 3072], P('fsdp')
- hidden_bias_grad: float32 [3072], P('fsdp')
- down_proj_grad: float32 [3072, 768], P('fsdp')
- down_bias_grad: float32 [768], P('fsdp')
Inputs may be any that keep to these rules, and one draw needn't show every extreme that they name: Rows 0 to counts[i] of image i hold its class token and visible patches; the rest of its 64 rows are padding.
All inputs are finite; a program needn't handle non-finite values.
Results may differ from a plain program's by a relative error of at most 0.015.
Values may be sent and summed in bfloat16 or wider, within the bound.
No kernel may reach another device: no remote copies, remote signals or barrier semaphores. Data moves between devices by JAX's collectives and lax.ppermute only.
A program may use at most 256 MiB of HBM per device.

v0:
```python
import functools
import jax
import jax.numpy as jnp
from jax import lax
from jax.experimental import pallas as pl
from jax.experimental.pallas import tpu as pltpu
from jax.sharding import PartitionSpec as P

HEADS = 12
HEAD = 64
EPS = 1e-06
BF = jnp.bfloat16
F32 = jnp.float32
VMEM = 63 << 20


def dot(a, b):
    return jnp.dot(a, b, preferred_element_type=F32)


def dot_rt(a, b):
    return lax.dot_general(a, b, (((1,), (1,)), ((), ())), preferred_element_type=F32)


def dot_lt(a, b):
    return lax.dot_general(a, b, (((0,), (0,)), ((), ())), preferred_element_type=F32)


def norm_stats(v):
    center = v - jnp.mean(v, axis=-1, keepdims=True)
    inv = lax.rsqrt(jnp.mean(center * center, axis=-1, keepdims=True) + EPS)
    return center, inv


def params(**kw):
    return pltpu.CompilerParams(vmem_limit_bytes=VMEM, **kw)


def full(shape):
    zeros = (0,) * len(shape)
    return pl.BlockSpec(shape, lambda *_: zeros, pipeline_mode=pl.Buffered(buffer_count=1))


def columns_of(rows, block, width):
    return pl.BlockSpec((rows, width), lambda *_: (0, block), pipeline_mode=pl.Buffered(buffer_count=1))


def pack_mlp_kernel(up, down, o_ref):
    rows, ff = up.shape
    width = ff // 4
    o_ref[:, :ff] = up[...]
    for j in range(4):
        o_ref[:, ff + j * width:ff + (j + 1) * width] = down[j * rows:(j + 1) * rows]


def pack_mlp(up, down):
    rows, ff = up.shape
    vm = pl.BlockSpec(memory_space=pltpu.VMEM)
    return pl.pallas_call(
        pack_mlp_kernel,
        in_specs=[vm, vm],
        out_specs=vm,
        out_shape=jax.ShapeDtypeStruct((rows, 2 * ff), BF),
        compiler_params=params(),
        name="pack_mlp",
    )(up, down)


def split_heads(pair, left):
    zero = jnp.zeros_like(pair)
    return jnp.concatenate([jnp.where(left, pair, zero), jnp.where(left, zero, pair)], axis=0)


def cost(flops, nbytes):
    return pl.CostEstimate(flops=int(flops), bytes_accessed=int(nbytes), transcendentals=0)


GROUPS = 16


def position(hier):
    if not hier:
        return 0, 0, 0
    me = lax.axis_index("fsdp")
    return me // 4, (me // 2) % 2, me % 2


def owner(hier, pos, k, other_x, other_c):
    if not hier:
        return (k * 2 + other_x) * 2 + other_c
    z, x, c = pos
    z = lax.rem(z + k, 4)
    x = 1 - x if other_x else x
    c = 1 - c if other_c else c
    return (z * 2 + x) * 2 + c


def rows_of(slot, rows):
    return pl.ds(pl.multiple_of(slot * rows, rows), rows)


def piece_copies(hier, mine, other, w_ref, sems, cols):
    pos = position(hier)
    out = []
    for c, ref in enumerate((mine, other)):
        for x in range(2):
            for k in range(4):
                slot = owner(hier, pos, (4 - k) % 4, x, c)
                out.append(pltpu.make_async_copy(ref.at[x * 4 + k, :, cols], w_ref.at[rows_of(slot, ref.shape[1])], sems.at[len(out)]))
    return out


def run_copies(copies):
    for copy in copies:
        copy.start()
    for copy in copies:
        copy.wait()


def pack_kernel(*refs):
    *vectors, hidden, in_proj, out_proj, o_ref, half_ref = refs
    rows = o_ref.shape[0]
    wide = in_proj.shape[1] + out_proj.shape[1]
    o_ref[:, :in_proj.shape[1]] = in_proj[...]
    o_ref[:, in_proj.shape[1]:wide] = out_proj[...]
    lines = [v[...].astype(F32).reshape(1, rows) for v in vectors]
    lines.insert(3, jnp.zeros((1, rows), F32))
    hidden = hidden[...].astype(F32).reshape(1, 4 * rows)
    lines += [hidden[:, j * rows:(j + 1) * rows] for j in range(4)] + [jnp.zeros((115, rows), F32)]
    o_ref[:, wide:wide + 128] = jnp.concatenate(lines, axis=0).T.astype(BF)
    o_ref[:, wide + 128:] = jnp.zeros((rows, 128), BF)
    some = half_ref.shape[1]
    half_ref[...] = o_ref[:, pl.ds(pl.multiple_of(lax.axis_index("rep") * some, 128), some)]


def pack(vectors, hidden, in_proj, out_proj):
    rows = in_proj.shape[0]
    wide = in_proj.shape[1] + out_proj.shape[1] + 256
    vm = pl.BlockSpec(memory_space=pltpu.VMEM)
    return pl.pallas_call(
        pack_kernel,
        in_specs=[vm] * (len(vectors) + 3),
        out_specs=[vm, vm],
        out_shape=[jax.ShapeDtypeStruct((rows, wide), BF), jax.ShapeDtypeStruct((rows, wide // 2), BF)],
        compiler_params=params(),
        name="pack",
    )(*vectors, hidden, in_proj, out_proj)


def assemble_kernel(own, across, *refs):
    *halves, o_ref = refs
    some = o_ref.shape[2] // 2
    rep = lax.axis_index("rep")
    here = pl.ds(pl.multiple_of(rep * some, 128), some)
    there = pl.ds(pl.multiple_of((1 - rep) * some, 128), some)
    o_ref[0] = own[...]
    o_ref[4] = across[...]
    for i in range(6):
        to = i + 1 if i < 3 else i + 2
        o_ref[to, :, here] = halves[2 * i][...]
        o_ref[to, :, there] = halves[2 * i + 1][...]


def assemble(own, across, halves):
    vm = pl.BlockSpec(memory_space=pltpu.VMEM)
    return pl.pallas_call(
        assemble_kernel,
        in_specs=[vm] * 14,
        out_specs=vm,
        out_shape=jax.ShapeDtypeStruct((8,) + own.shape, BF),
        compiler_params=params(),
        name="assemble",
    )(own, across, *halves)


def pair_cols(width, p):
    return [slice(j * width + p * 128, j * width + (p + 1) * 128) for j in range(3)]


def attn_fwd_kernel(chunk, hier, counts, x_ref, cot_ref, mine, other,
                    qkv_ref, probs_ref, att_ref, mid_ref, sec_ref, back_ref, db_ref, vec, w_ref, sems):
    step = pl.program_id(0)
    rows, width = x_ref.shape
    per = rows // 64

    @pl.when(step == 0)
    def _():
        run_copies(piece_copies(hier, mine, other, w_ref, sems, slice(None)))
        vec[...] = w_ref[:, 4 * width:4 * width + 128].astype(F32).T[:16]
        db_ref[...] = jnp.zeros_like(db_ref)

    left = lax.broadcasted_iota(jnp.int32, (64, 128), 1) < HEAD
    row = lax.broadcasted_iota(jnp.int32, (64, 128), 0)
    pos = lax.broadcasted_iota(jnp.int32, (64, width), 0)

    def project(at):
        center, inv = norm_stats(x_ref[at].astype(F32))
        first = (center * inv * vec[0:1] + vec[1:2]).astype(BF)
        for j in range(3):
            cols = slice(j * width, (j + 1) * width)
            qkv_ref[at, cols] = (dot(first, w_ref[:, cols]) + vec[2 + j:3 + j]).astype(BF)

    def attend(at):
        work = []
        for i in range(at.start // 64, at.stop // 64):
            here = slice(i * 64, (i + 1) * 64)
            work += [(i, here, row <= counts[step * per + i], pair_cols(width, p), p) for p in range(HEADS // 2)]
        scores = [dot_rt(qkv_ref[here, c[1]], split_heads(qkv_ref[here, c[0]], left)) for i, here, usable, c, p in work]
        lows = []
        for (i, here, usable, c, p), s in zip(work, scores):
            s = jnp.where(usable, s * 0.125, -1000000000.0)
            e = jnp.exp(s - jnp.max(s, axis=0, keepdims=True))
            low = (e * (1.0 / jnp.sum(e, axis=0, keepdims=True))).astype(BF)
            probs_ref[i, p] = low
            lows.append(low)
        for (i, here, usable, c, p), low in zip(work, lows):
            o = dot_lt(low, qkv_ref[here, c[2]])
            att_ref[here, c[0]] = jnp.where(left, o[:64], o[64:]).astype(BF)

    def output(at):
        mid = x_ref[at].astype(F32) + dot(att_ref[at], w_ref[:, 3 * width:4 * width]) + vec[5:6]
        mid_ref[at] = mid
        center, inv = norm_stats(mid)
        sec_ref[at] = (center * inv * vec[6:7] + vec[7:8]).astype(BF)

    chunks = [slice(r, r + chunk) for r in range(0, rows, chunk)]
    project(chunks[0])
    for c, at in enumerate(chunks):
        if c + 1 < len(chunks):
            project(chunks[c + 1])
        attend(at)
        output(at)
    total = jnp.zeros((1, width), F32)
    for i in range(per):
        at = slice(i * 64, (i + 1) * 64)
        back = jnp.where(pos <= counts[step * per + i], cot_ref[at].astype(F32), 0.0)
        back_ref[at] = back.astype(BF)
        total = total + jnp.sum(back, axis=0, keepdims=True)
    db_ref[...] += total


ANY = pl.BlockSpec(memory_space=pl.ANY)


def attn_fwd(hier, counts, x, cot, mine, other, rows=512, chunk=256):
    total, width = x.shape
    per = rows // 64
    blk = lambda w: pl.BlockSpec((rows, w), lambda i: (i, 0))
    return pl.pallas_call(
        functools.partial(attn_fwd_kernel, chunk, hier),
        grid=(total // rows,),
        in_specs=[pl.BlockSpec(memory_space=pltpu.SMEM), blk(width), blk(width), ANY, ANY],
        out_specs=[blk(3 * width), pl.BlockSpec((per, HEADS // 2, 64, 128), lambda i: (i, 0, 0, 0)),
                   blk(width), blk(width), blk(width), blk(width), pl.BlockSpec((1, width), lambda i: (0, 0)),
                   pl.BlockSpec((16, width), lambda i: (0, 0))],
        out_shape=[jax.ShapeDtypeStruct((total, 3 * width), BF),
                   jax.ShapeDtypeStruct((total // 64, HEADS // 2, 64, 128), BF),
                   jax.ShapeDtypeStruct((total, width), BF),
                   jax.ShapeDtypeStruct((total, width), F32),
                   jax.ShapeDtypeStruct((total, width), BF),
                   jax.ShapeDtypeStruct((total, width), BF),
                   jax.ShapeDtypeStruct((1, width), F32),
                   jax.ShapeDtypeStruct((16, width), F32)],
        scratch_shapes=[pltpu.VMEM((width, mine.shape[2]), BF), pltpu.SemaphoreType.DMA((GROUPS,))],
        compiler_params=params(),
        cost_estimate=cost(8 * total * width * width * 1.5, 20 * total * width),
        name="attn_fwd",
    )(counts, x, cot, mine, other)


def gelu_parts(h):
    cdf = 0.5 + 0.5 * lax.erf(h * 0.7071067811865476)
    pdf = jnp.exp(h * h * -0.5) * 0.3989422804014327
    return (h * cdf).astype(BF), cdf + h * pdf


def whole_rows(packed):
    owners, rows, four = packed.shape
    width = four // 4
    return jnp.concatenate([packed[o, :, j * width:(j + 1) * width] for o in range(owners) for j in range(4)], axis=0)


def mlp_kernel(chunk, sec_ref, back_ref, bias_ref, up, down, act_hbm, hg_hbm, hb_ref, g_hbm,
               act_ref, hg_ref, ug_ref, dg_ref, a_sems, g_sems):
    step = pl.program_id(0)
    last = pl.num_programs(0) - 1
    rows, width = sec_ref.shape
    owners, part, ff = dg_ref.shape
    slot = lax.rem(step, 2)

    def blocks(s, which):
        at = pl.ds(pl.multiple_of(s * width, width), width)
        return (pltpu.make_async_copy(act_ref.at[which], act_hbm.at[:, at], a_sems.at[which, 0]),
                pltpu.make_async_copy(hg_ref.at[which], hg_hbm.at[:, at], a_sems.at[which, 1]))

    def outputs(s):
        at = pl.ds(pl.multiple_of(s * width, width), width)
        return (pltpu.make_async_copy(dg_ref, g_hbm.at[pl.ds(s * owners, owners), :, ff:], g_sems.at[0]),
                pltpu.make_async_copy(ug_ref, g_hbm.at[:, :, at], g_sems.at[1]))

    @pl.when(step > 1)
    def _():
        for copy in blocks(step - 2, slot):
            copy.wait()

    @pl.when(step > 0)
    def _():
        for copy in outputs(step - 1):
            copy.wait()

    down = whole_rows(down)
    sums = jnp.zeros((8, width), F32)
    for r in range(rows // chunk):
        at = slice(r * chunk, (r + 1) * chunk)
        act, slope = gelu_parts(dot(sec_ref[at], up[...]) + bias_ref[...])
        act_ref[slot, at] = act
        hg = (dot_rt(back_ref[at], down) * slope).astype(BF)
        hg_ref[slot, at] = hg
        sums = sums + jnp.sum(hg.astype(F32).reshape(chunk // 8, 8, -1), axis=0)
    for copy in blocks(step, slot):
        copy.start()
    column = jnp.sum(jnp.concatenate([sums, jnp.zeros((120, width), F32)], axis=0).T, axis=1, keepdims=True)
    lane = lax.broadcasted_iota(jnp.int32, (part, 128), 1)
    for o in range(owners):
        rows_j = [column[(o * 4 + j) * part:(o * 4 + j + 1) * part] for j in range(4)]
        hb_ref[o * part:(o + 1) * part] = sum(jnp.where(lane == 12 + j, rows_j[j], 0.0) for j in range(4))
    dg = dot_lt(act_ref[slot], back_ref[...]).astype(BF)
    for o in range(owners):
        for j in range(4):
            dg_ref[o, :, j * width:(j + 1) * width] = dg[(o * 4 + j) * part:(o * 4 + j + 1) * part]
    outputs(step)[0].start()
    ug_ref[...] = dot_lt(sec_ref[...], hg_ref[slot]).astype(BF).reshape(ug_ref.shape)
    outputs(step)[1].start()

    @pl.when(step == last)
    def _():
        for copy in blocks(step - 1, 1 - slot) + blocks(step, slot) + outputs(step):
            copy.wait()


def mlp(sec, back, bias, updown, chunk=256):
    total, width = sec.shape
    ff = bias.shape[1]
    f = width
    part = width // GROUPS
    owners = GROUPS * f // ff
    col = lambda r: pl.BlockSpec((r, f), lambda i: (0, i))
    return pl.pallas_call(
        functools.partial(mlp_kernel, chunk),
        grid=(ff // f,),
        in_specs=[full(sec.shape), full(back.shape), col(1), col(width),
                  pl.BlockSpec((owners, part, ff), lambda i: (i, 0, 1))],
        out_specs=[ANY, ANY, pl.BlockSpec((owners * part, 128), lambda i: (i, 0)), ANY],
        out_shape=[jax.ShapeDtypeStruct((total, ff), BF), jax.ShapeDtypeStruct((total, ff), BF),
                   jax.ShapeDtypeStruct((width, 128), F32), jax.ShapeDtypeStruct((GROUPS, part, 2 * ff), BF)],
        scratch_shapes=[pltpu.VMEM((2, total, f), BF), pltpu.VMEM((2, total, f), BF), pltpu.VMEM((GROUPS, part, f), BF),
                        pltpu.VMEM((owners, part, ff), BF), pltpu.SemaphoreType.DMA((2, 2)), pltpu.SemaphoreType.DMA((2,))],
        compiler_params=params(),
        cost_estimate=cost(8 * total * width * ff, 12 * total * width),
        name="mlp",
    )(sec, back, bias, updown, updown.reshape(GROUPS, part, 2 * ff))


def attn_bwd_kernel(hier, hg_ref, mid_ref, back_ref, att_ref, qkv_ref, probs_ref, x_ref, vec, up, db_ref, hid_ref, mine, other,
                    mg_ref, qg_ref, near_hbm, far_hbm, out_acc, in_acc, sums, cs, ag_ref, low_ref, payload, w_ref, sems, out_sems):
    step = pl.program_id(0)
    steps = pl.num_programs(0) - 1
    rows, width = mid_ref.shape

    @pl.when(step == 0)
    def _():
        for copy in piece_copies(hier, mine, other, w_ref, sems, slice(None)):
            copy.start()
        for ref in (out_acc, in_acc, sums, cs):
            ref[...] = jnp.zeros_like(ref)

    left = lax.broadcasted_iota(jnp.int32, (64, 128), 1) < HEAD

    def body(here_too, before_too):
        if before_too:
            center, inv = norm_stats(x_ref[...].astype(F32))
            first = (center * inv).astype(BF)
            work = []
            for i in range(rows // 64):
                work += [(i, slice(i * 64, (i + 1) * 64), pair_cols(width, p), p) for p in range(HEADS // 2)]
            dps = []
            for i, here, c, p in work:
                da = split_heads(ag_ref[here, c[0]], left)
                qg_ref[here, c[2]] = dot(probs_ref[i, p], da).astype(BF)
                dps.append(dot_rt(qkv_ref[here, c[2]], da))
            dss = []
            for (i, here, c, p), dp in zip(work, dps):
                pr = probs_ref[i, p].astype(F32)
                t = dp * pr
                dss.append((t - pr * jnp.sum(t, axis=0, keepdims=True)).astype(BF))
            for (i, here, c, p), ds in zip(work, dss):
                qg_ref[here, c[1]] = (dot(ds, split_heads(qkv_ref[here, c[0]], left)) * 0.125).astype(BF)
                dq = dot_lt(ds, qkv_ref[here, c[1]])
                qg_ref[here, c[0]] = (jnp.where(left, dq[:64], dq[64:]) * 0.125).astype(BF)
        if here_too:
            sg = dot_rt(hg_ref[...], up[...])
        if before_too:
            out_acc[...] += dot_lt(att_ref[...], low_ref[...])
        if here_too:
            center, inv = norm_stats(mid_ref[...])
            n = center * inv
            e = sg * vec[6:7]
        if before_too:
            for j in range(3):
                cols = slice(j * width, (j + 1) * width)
                in_acc[:, cols] += dot_lt(first, qg_ref[:, cols])
                cs[:, cols] += jnp.sum(qg_ref[:, cols].astype(F32), axis=0, keepdims=True)
        if here_too:
            norm_grad = inv * (e - jnp.mean(e, axis=-1, keepdims=True) - n * jnp.mean(e * n, axis=-1, keepdims=True))
            mg = back_ref[...].astype(F32) + norm_grad
            mg_ref[...] = mg
            sums[0:1] += jnp.sum(sg * n, axis=0, keepdims=True)
            sums[1:2] += jnp.sum(sg, axis=0, keepdims=True)
            sums[2:3] += jnp.sum(mg, axis=0, keepdims=True)
            low = mg.astype(BF)
            low_ref[...] = low
            if not before_too:
                for copy in piece_copies(hier, mine, other, w_ref, sems, slice(None)):
                    copy.wait()
            ag_ref[...] = dot_rt(low, w_ref[:, 3 * width:4 * width]).astype(BF)

    @pl.when(step == 0)
    def _():
        body(True, False)

    @pl.when((step > 0) & (step < steps))
    def _():
        body(True, True)

    @pl.when(step == steps)
    def _():
        body(False, True)

    @pl.when(step == steps)
    def _():
        pos = position(hier)
        sent = []

        def send(cols):
            for away, ref in enumerate((near_hbm, far_hbm)):
                for x in range(2):
                    for k in range(4):
                        copy = pltpu.make_async_copy(payload.at[owner(hier, pos, k, x, away), :, cols], ref.at[x, k, :, cols],
                                                     out_sems.at[len(sent)])
                        copy.start()
                        sent.append(copy)

        def hold(cols, value):
            payload[:, :, cols] = value.astype(BF).reshape(payload.shape[0], payload.shape[1], cols.stop - cols.start)
            send(cols)

        hold(slice(3 * width, 4 * width), out_acc[...])
        tail = w_ref[:, 4 * width:4 * width + 128].astype(F32)
        gain, shift = tail[:, 0:1], tail[:, 1:2]
        gain_grad = jnp.zeros((width, 1), F32)
        shift_grad = jnp.zeros((width, 1), F32)
        for j in range(3):
            cols = slice(j * width, (j + 1) * width)
            w = w_ref[:, cols].astype(F32)
            hold(cols, gain * in_acc[:, cols] + shift * cs[:, cols])
            gain_grad = gain_grad + jnp.sum(w * in_acc[:, cols], axis=1, keepdims=True)
            shift_grad = shift_grad + jnp.sum(w * cs[:, cols], axis=1, keepdims=True)
        lines = jnp.concatenate([db_ref[...], sums[0:3], cs[:, :width], cs[:, 2 * width:], jnp.zeros((122, width), F32)], axis=0)
        lane = lax.broadcasted_iota(jnp.int32, (width, 128), 1)
        last = jnp.where(lane == 10, gain_grad, jnp.where(lane == 11, shift_grad, jnp.where(lane < 10, lines.T, hid_ref[...])))
        hold(slice(4 * width, 4 * width + 256), jnp.concatenate([last, jnp.zeros_like(last)], axis=1))
        for copy in sent:
            copy.wait()


def attn_bwd(hier, hg, mid, back, att, qkv, probs, x, vec, updown, db, hid, mine, other, rows=256):
    total, width = mid.shape
    ff = hg.shape[1]
    per = rows // 64
    wide = 4 * width + 256
    part = width // GROUPS
    steps = total // rows
    now = lambda w: pl.BlockSpec((rows, w), lambda i: (jnp.minimum(i, steps - 1), 0))
    ago = lambda w: pl.BlockSpec((rows, w), lambda i: (jnp.maximum(i - 1, 0), 0))
    return pl.pallas_call(
        functools.partial(attn_bwd_kernel, hier),
        grid=(steps + 1,),
        in_specs=[now(ff), now(width), now(width), ago(width), ago(3 * width),
                  pl.BlockSpec((per, HEADS // 2, 64, 128), lambda i: (jnp.maximum(i - 1, 0), 0, 0, 0)), ago(width),
                  full(vec.shape), columns_of(width, 0, ff), full(db.shape), full(hid.shape), ANY, ANY],
        out_specs=[now(width), ago(3 * width), ANY, ANY],
        out_shape=[jax.ShapeDtypeStruct((total, width), F32), jax.ShapeDtypeStruct((total, 3 * width), BF),
                   jax.ShapeDtypeStruct((2, 4, part, wide), BF), jax.ShapeDtypeStruct((2, 4, part, wide), BF)],
        scratch_shapes=[pltpu.VMEM((width, width), F32), pltpu.VMEM((width, 3 * width), F32), pltpu.VMEM((8, width), F32),
                        pltpu.VMEM((1, 3 * width), F32), pltpu.VMEM((rows, width), BF), pltpu.VMEM((rows, width), BF),
                        pltpu.VMEM((GROUPS, part, wide), BF), pltpu.VMEM((width, mine.shape[2]), BF), pltpu.SemaphoreType.DMA((GROUPS,)),
                        pltpu.SemaphoreType.DMA((5 * GROUPS,))],
        compiler_params=params(),
        cost_estimate=cost(2 * total * width * (ff + 9 * width), 28 * total * width),
        name="attn_bwd",
    )(hg, mid, back, att, qkv, probs, x, vec, updown, db, hid, mine, other)


def tokens_grad_kernel(hier, x_ref, qg_ref, mg_ref, vec, mine, other, tie, old, o_ref, w_ref, sems):
    @pl.when(pl.program_id(0) == 0)
    def _():
        run_copies(piece_copies(hier, mine, other, w_ref, sems, slice(0, w_ref.shape[1])))

    center, inv = norm_stats(x_ref[...].astype(F32))
    n = center * inv
    e = dot_rt(qg_ref[...], w_ref[...]) * vec[0:1]
    grad = inv * (e - jnp.mean(e, axis=-1, keepdims=True) - n * jnp.mean(e * n, axis=-1, keepdims=True))
    o_ref[...] = (mg_ref[...] + grad).astype(BF)


def part_of(rows, first, width):
    return pl.BlockSpec((rows, width), lambda i: (first + i, 0))


def tokens_grad(hier, first, blocks, x, qg, mg, vec, mine, other, tie, old, rows=256):
    total, width = x.shape
    blk = lambda w: part_of(rows, first, w)
    return pl.pallas_call(
        functools.partial(tokens_grad_kernel, hier),
        grid=(blocks,),
        in_specs=[blk(width), blk(3 * width), blk(width), full(vec.shape), ANY, ANY, ANY, ANY],
        out_specs=blk(width),
        out_shape=jax.ShapeDtypeStruct((total, width), BF),
        scratch_shapes=[pltpu.VMEM((width, 3 * width), BF), pltpu.SemaphoreType.DMA((GROUPS,))],
        input_output_aliases={7: 0} if first else {},
        compiler_params=params(),
        cost_estimate=cost(6 * blocks * rows * width * width, 14 * blocks * rows * width),
        name="tokens_grad",
    )(x, qg, mg, vec, mine, other, tie, old)


def mixed_kernel(first, counts, act_ref, mid_ref, vec, down, tie, old, o_ref):
    step = pl.program_id(0)
    per = o_ref.shape[0] // 64
    r = mid_ref[...] + dot(act_ref[...], whole_rows(down)) + vec[8:9]
    pos = lax.broadcasted_iota(jnp.int32, (64, o_ref.shape[1]), 0)
    for i in range(per):
        count = counts[(first + step) * per + i]
        o_ref[i * 64:(i + 1) * 64] = jnp.where(pos <= count, r[i * 64:(i + 1) * 64], 0.0).astype(BF)


def mixed_out(first, blocks, counts, act, mid, vec, updown, tie, old, rows=256):
    total, width = mid.shape
    ff = act.shape[1]
    blk = lambda w: part_of(rows, first, w)
    packed = updown.reshape(GROUPS, width // GROUPS, 2 * ff)
    return pl.pallas_call(
        functools.partial(mixed_kernel, first),
        grid=(blocks,),
        in_specs=[pl.BlockSpec(memory_space=pltpu.SMEM), blk(ff), blk(width), full(vec.shape),
                  pl.BlockSpec((GROUPS, width // GROUPS, ff), lambda i: (0, 0, 1), pipeline_mode=pl.Buffered(buffer_count=1)), ANY, ANY],
        out_specs=blk(width),
        out_shape=jax.ShapeDtypeStruct((total, width), BF),
        input_output_aliases={6: 0} if first else {},
        compiler_params=params(),
        cost_estimate=cost(2 * blocks * rows * width * ff, 14 * blocks * rows * width),
        name="mixed",
    )(counts, act, mid, vec, packed, tie, old)


FIRST = 512
SECOND = 1152


def add(a, b):
    return (a.astype(F32) + b.astype(F32)).astype(BF)


def core_sum_kernel(near, got, x_keep, x_send, y_keep, y_send):
    rep = lax.axis_index("rep")
    first = slice(0, 2 * FIRST)
    x_keep[0] = add(near[0, 0, :, first], got[0, 0, :, first])
    x_send[0] = add(near[1, 0, :, first], got[1, 0, :, first])
    for x in range(2):
        for ref, half in ((y_keep, rep), (y_send, 1 - rep)):
            at = pl.ds(pl.multiple_of(2 * FIRST + half * SECOND, 128), SECOND)
            ref[x, 0] = add(near[x, 0, :, at], got[x, 0, :, at])


def core_sum(near, got):
    _, along, rows, wide = near.shape
    blk = pl.BlockSpec((2, 1, rows, wide), lambda i: (0, i, 0, 0))
    one = pl.BlockSpec((1, rows, 2 * FIRST), lambda i: (i, 0, 0))
    two = pl.BlockSpec((2, 1, rows, SECOND), lambda i: (0, i, 0, 0))
    return pl.pallas_call(
        core_sum_kernel,
        grid=(along,),
        in_specs=[blk, blk],
        out_specs=[one, one, two, two],
        out_shape=[jax.ShapeDtypeStruct((along, rows, 2 * FIRST), BF)] * 2 + [jax.ShapeDtypeStruct((2, along, rows, SECOND), BF)] * 2,
        compiler_params=params(),
        name="core_sum",
    )(near, got)


def across_sum_kernel(x_keep, x_got, y_keep, y_got, tie, first_keep, first_send, second_keep, second_send):
    rep = lax.axis_index("rep")
    for ref, half in ((first_keep, rep), (first_send, 1 - rep)):
        at = pl.ds(pl.multiple_of(half * FIRST, 128), FIRST)
        ref[...] = add(x_keep[:, :, at], x_got[:, :, at])
    second_keep[...] = add(y_keep[0], y_got[0])
    second_send[...] = add(y_keep[1], y_got[1])


def across_sum(x_keep, x_got, y_keep, y_got, tie):
    along, rows, _ = x_keep.shape
    vm = pl.BlockSpec(memory_space=pltpu.VMEM)
    return pl.pallas_call(
        across_sum_kernel,
        in_specs=[vm] * 4 + [ANY],
        out_specs=[vm] * 4,
        out_shape=[jax.ShapeDtypeStruct((along, rows, FIRST), BF)] * 2 + [jax.ShapeDtypeStruct((along, rows, SECOND), BF)] * 2,
        compiler_params=params(),
        name="across_sum",
    )(x_keep, x_got, y_keep, y_got, tie)


def plane_sum_kernel(first_keep, first_got, second_keep, second_got, tie, *outs):
    for k, o_ref in enumerate(outs):
        o_ref[:, :FIRST] = add(first_keep[k], first_got[k])
        o_ref[:, FIRST:] = add(second_keep[k], second_got[k])


def plane_sum(first_keep, first_got, second_keep, second_got, tie):
    along, rows, _ = first_keep.shape
    vm = pl.BlockSpec(memory_space=pltpu.VMEM)
    return pl.pallas_call(
        plane_sum_kernel,
        in_specs=[vm] * 4 + [ANY],
        out_specs=[vm] * along,
        out_shape=[jax.ShapeDtypeStruct((rows, FIRST + SECOND), BF)] * along,
        compiler_params=params(),
        name="plane_sum",
    )(first_keep, first_got, second_keep, second_got, tie)


def along_sum_kernel(a, b, c, d, tie, o_ref):
    total = (a[...].astype(F32) + b[...].astype(F32)) + (c[...].astype(F32) + d[...].astype(F32))
    o_ref[...] = total.astype(BF)


def along_sum(a, b, c, d, tie):
    vm = pl.BlockSpec(memory_space=pltpu.VMEM)
    return pl.pallas_call(
        along_sum_kernel,
        in_specs=[vm] * 4 + [ANY],
        out_specs=vm,
        out_shape=jax.ShapeDtypeStruct(a.shape, BF),
        compiler_params=params(),
        name="along_sum",
    )(a, b, c, d, tie)


def finish_kernel(a_ref, b_ref, tie, in_ref, out_ref, *vectors):
    rows = a_ref.shape[0]
    front = lax.axis_index("rep") == 0
    a, b = a_ref[...].astype(F32), b_ref[...].astype(F32)
    low, high = jnp.where(front, a, b), jnp.where(front, b, a)
    total = jnp.concatenate([low[:, :FIRST], high[:, :FIRST], low[:, FIRST:], high[:, FIRST:]], axis=1)
    wide = in_ref.shape[1] + out_ref.shape[1]
    in_ref[...] = total[:, :in_ref.shape[1]]
    out_ref[...] = total[:, in_ref.shape[1]:wide]
    lines = total[:, wide:wide + 128].T
    for i, v in enumerate(vectors[:-1]):
        v[...] = lines[i:i + 1].reshape(rows)
    hidden = jnp.concatenate([lines[12 + j:13 + j] for j in range(4)], axis=1)
    vectors[-1][...] = hidden.reshape(4 * rows)


def finish(a, b, tie, width):
    rows = a.shape[0]
    vm = pl.BlockSpec(memory_space=pltpu.VMEM)
    return pl.pallas_call(
        finish_kernel,
        in_specs=[vm, vm, ANY],
        out_specs=[vm] * 15,
        out_shape=[jax.ShapeDtypeStruct((rows, 3 * width), F32), jax.ShapeDtypeStruct((rows, width), F32)]
        + [jax.ShapeDtypeStruct((rows,), F32)] * 12 + [jax.ShapeDtypeStruct((4 * rows,), F32)],
        compiler_params=params(),
        name="finish",
    )(a, b, tie)


def finish_mlp_kernel(a_ref, b_ref, tie, up_ref, down_ref):
    rows, ff = up_ref.shape
    width = ff // 4
    total = a_ref[...].astype(F32) + b_ref[...].astype(F32)
    up_ref[...] = total[:, :ff]
    for j in range(4):
        down_ref[j * rows:(j + 1) * rows] = total[:, ff + j * width:ff + (j + 1) * width]


def finish_mlp(a, b, tie):
    rows, wide = a.shape
    vm = pl.BlockSpec(memory_space=pltpu.VMEM)
    return pl.pallas_call(
        finish_mlp_kernel,
        in_specs=[vm, vm, ANY],
        out_specs=[vm, vm],
        out_shape=[jax.ShapeDtypeStruct((rows, wide // 2), F32), jax.ShapeDtypeStruct((4 * rows, wide // 8), F32)],
        compiler_params=params(),
        name="finish_mlp",
    )(a, b, tie)


CORE = [(i, i ^ 1) for i in range(16)]
ACROSS = [(i, i ^ 2) for i in range(16)]
ALONG = [[(i, ((i // 4 + k) % 4) * 4 + i % 4) for i in range(16)] for k in range(4)]
SWAP = [(0, 1), (1, 0)]


def permute(v, pairs):
    return lax.ppermute(v, "fsdp", pairs)


def gather_pieces(whole, half):
    swap = lambda v: lax.ppermute(v, "rep", SWAP)
    across = permute(whole, ACROSS)
    along = {k: permute(half, ALONG[k]) for k in (1, 3, 2)}
    both = {k: permute(along[k], ACROSS) for k in (1, 3, 2)}
    halves = []
    for k in (1, 2, 3):
        halves += [along[k], swap(along[k])]
    for k in (1, 2, 3):
        halves += [both[k], swap(both[k])]
    mine = assemble(whole, across, halves)
    return mine, permute(mine, CORE)


def gather_whole(shard):
    whole = lax.all_gather(shard, "fsdp", axis=0, tiled=True)
    whole = whole.reshape(4, 2, 2, whole.shape[0] // GROUPS, whole.shape[1])
    order = jnp.concatenate([whole[:1], whole[3:0:-1]], axis=0).transpose(2, 1, 0, 3, 4)
    return order[0].reshape((8,) + order.shape[3:]), order[1].reshape((8,) + order.shape[3:])


def regroup(updown, own):
    width = updown.shape[0]
    ff = 4 * width
    down = updown[:, ff:].reshape(width // own, own, 4, width).transpose(0, 2, 1, 3).reshape(GROUPS, 4, width // GROUPS, width)
    return jnp.concatenate([updown[:, :ff], down.transpose(0, 2, 1, 3).reshape(width, ff)], axis=1)


def over_rep(shard):
    low = shard.astype(BF)
    return low, lax.ppermute(low, "rep", SWAP)


def after(value, other):
    return lax.optimization_barrier((value, other))[0]


def local(hier, tokens, counts, cotangent, first_gain, first_shift, in_proj, query_bias, value_bias, out_proj, out_bias,
          second_gain, second_shift, up_proj, hidden_bias, down_proj, down_bias):
    images, rows, width = tokens.shape
    own = first_gain.shape[0]
    ff = 4 * width
    x = tokens.reshape(images * rows, width)
    cot = cotangent.reshape(images * rows, width)
    vectors = (first_gain, first_shift, query_bias, value_bias, out_bias, second_gain, second_shift, down_bias)
    if hier:
        mine, other = gather_pieces(*pack(vectors, hidden_bias, in_proj, out_proj))
        updown = lax.all_gather(pack_mlp(up_proj, down_proj), "fsdp", axis=0, tiled=True)
    else:
        columns = jnp.concatenate(vectors[:3] + (jnp.zeros_like(query_bias),) + vectors[3:] + (hidden_bias,)).reshape(13, own).T
        packed = jnp.concatenate([in_proj, out_proj, columns, jnp.zeros((own, 243), BF)], axis=1)
        mine, other = gather_whole(packed)
        updown = jnp.concatenate([up_proj] + [down_proj[j * own:(j + 1) * own] for j in range(4)], axis=1)
        updown = regroup(lax.all_gather(updown, "fsdp", axis=0, tiled=True), own)
    qkv, probs, att, mid, sec, back, db, vec = attn_fwd(hier, counts, x, cot, mine, other)
    owners = width // own
    bias = vec[9:13].reshape(4, owners, own).transpose(1, 0, 2).reshape(1, ff)
    act, hg, hid, grads = mlp(sec, back, bias, updown)
    if not hier:
        sums = hid[:, 12:16].reshape(GROUPS, width // GROUPS, 4).transpose(0, 2, 1).reshape(owners, 4, own).transpose(0, 2, 1)
        hid = hid.at[:, 12:16].set(sums.reshape(width, 4))
        dg = grads[:, :, ff:].reshape(GROUPS, width // GROUPS, 4, width).transpose(0, 2, 1, 3).reshape(owners, 4, own, width)
        grads = jnp.concatenate([grads[:, :, :ff].reshape(width, ff), dg.transpose(0, 2, 1, 3).reshape(width, ff)], axis=1)
    mlp_grads = lax.psum_scatter(grads.reshape(width, 2 * ff), "fsdp", scatter_dimension=0, tiled=True)
    mg, qg, near, far = attn_bwd(hier, hg, mid, back, att, qkv, probs, x, vec, updown, db, hid, mine, other)
    blocks = images * rows // 256
    tok = lambda first, last, tie, old: tokens_grad(hier, first, last - first, x, qg, mg, vec, mine, other, tie, old)
    mix = lambda tie: mixed_out(0, blocks, counts, act, mid, vec, updown, tie, tie)
    if hier:
        got = permute(far, CORE)
        x_keep, x_send, y_keep, y_send = core_sum(near, got)
        x_got, y_got = permute(x_send, ACROSS), lax.ppermute(y_send, "rep", SWAP)
        mixed = mix(x_send)
        first_keep, first_send, second_keep, second_send = across_sum(x_keep, x_got, y_keep, y_got, mixed)
        first_got, second_got = lax.ppermute(first_send, "rep", SWAP), permute(second_send, ACROSS)
        toks = tok(0, blocks // 2, first_send, mixed)
        parts = plane_sum(first_keep, first_got, second_keep, second_got, toks)
        moved = [permute(after(parts[k], mlp_grads), ALONG[k]) for k in (2, 1, 3)]
        toks = tok(blocks // 2, blocks, parts[3], toks)
        mlp_grads = after(mlp_grads, parts[3])
        mlp_got = lax.ppermute(mlp_grads, "rep", SWAP)
        low = along_sum(parts[0], *moved, toks)
        grad_up, grad_down = finish_mlp(mlp_grads, mlp_got, low)
        grad_in, grad_out, *lines, hidden = finish(low, lax.ppermute(low, "rep", SWAP), grad_up, width)
    else:
        mixed = mix(far)
        toks = tok(0, blocks, far, far)
        pieces = jnp.stack([near, far]).transpose(2, 1, 0, 3, 4).reshape(width, near.shape[-1])
        a, b = over_rep(lax.psum_scatter(pieces, "fsdp", scatter_dimension=0, tiled=True))
        wide = a.astype(F32) + b.astype(F32)
        grad_in, grad_out, lines = wide[:, :3 * width], wide[:, 3 * width:4 * width], wide[:, 4 * width:].T
        hidden = lines[12:16].reshape(4 * own)
        a, b = over_rep(mlp_grads)
        mlp_grads = a.astype(F32) + b.astype(F32)
        grad_up = mlp_grads[:, :ff]
        grad_down = jnp.concatenate([mlp_grads[:, ff + j * width:ff + (j + 1) * width] for j in range(4)], axis=0)
    return (mixed.reshape(tokens.shape), toks.reshape(tokens.shape), lines[10], lines[11], grad_in, lines[4], lines[5],
            grad_out, lines[3], lines[1], lines[2], grad_up, hidden, grad_down, lines[0])


def solution(mesh):
    rows = P(("fsdp", "rep"), None, None)
    v, m = P("fsdp"), P("fsdp", None)
    in_specs = (rows, P(("fsdp", "rep")), rows, v, v, m, v, v, m, v, v, v, m, v, m, v)
    out_specs = (rows, rows, v, v, m, v, v, m, v, v, v, m, v, m, v)
    hier = mesh.shape["fsdp"] == GROUPS and mesh.shape["rep"] == 2
    return jax.shard_map(functools.partial(local, hier), mesh=mesh, in_specs=in_specs, out_specs=out_specs, check_vma=False)
```

profile of v0, /device:TPU:0, one launch (start us, length us, event | category | flops | bytes accessed | tf_op | source)
XLA Modules:
  0.0 301.7 jit_solution(10225930238400932723)
XLA Ops:
  7.2 1.9 pack_mlp.1
  9.2 2.0 pack.1
  11.3 5.0 %collective-permute-start.5 = (bf16[48,1664]{1,0:T(8,128)(2,1)}, bf16[48,1664]{1,0:T(8,128)(2,1)S(1)}, u32[]{:S(2)}, u32[]{:S(2)}) collective-permute-start(bf16[48,1664]{1,0:T(8,128)(2,1)} %get-tuple-element.63), channel_id=1, source_target_pairs={{0,24},{2,26},{4,28},{6,30},{8,0},{10,2},{12,4},{14,6},{16,8},{18,... | collective-permute-start | bytes 479240 | tf_op jit(solution)/shard_map/ppermute | solution.py:718
  16.3 1.0 collective-permute-start.1
  17.3 3.9 %collective-permute-done.5.refs_4_ = bf16[48,1664]{1,0:T(8,128)(2,1)S(1)} collective-permute-done((bf16[48,1664]{1,0:T(8,128)(2,1)}, bf16[48,1664]{1,0:T(8,128)(2,1)S(1)}, u32[]{:S(2)}, u32[]{:S(2)}) %collective-permute-start.5) | collective-permute-done | bytes 159776 | tf_op jit(solution)/shard_map/ppermute | solution.py:718
  21.2 1.5 collective-permute-start.11
  23.2 1.5 collective-permute-start.6
  24.7 13.1 %collective-permute-done.3.refs_2_ = bf16[48,1664]{1,0:T(8,128)(2,1)S(1)} collective-permute-done((bf16[48,1664]{1,0:T(8,128)(2,1)}, bf16[48,1664]{1,0:T(8,128)(2,1)S(1)}, u32[]{:S(2)}, u32[]{:S(2)}) %collective-permute-start.3) | collective-permute-done | bytes 159776 | tf_op jit(solution)/shard_map/ppermute | solution.py:718
  37.8 2.2 collective-permute-start.9
  40.0 1.5 collective-permute-start.4
  42.1 1.7 collective-permute-done.9.refs_8_
  43.9 1.0 collective-permute-start.12
  44.9 2.1 collective-permute-done.4.refs_3_
  47.0 1.5 collective-permute-start.10
  49.0 1.4 collective-permute-done.2.refs_1_
  50.4 2.6 collective-permute-done.12.refs_11_
  53.0 1.7 collective-permute-done.10.refs_9_
  55.4 1.1 collective-permute-done.8.refs_7_
  56.6 3.5 %assemble.1.mine = bf16[8,48,3328]{2,1,0:T(8,128)(2,1)} custom-call(bf16[48,3328]{1,0:T(8,128)(2,1)} %get-tuple-element.62.own, bf16[48,3328]{1,0:T(8,128)(2,1)} %copy-done.3, bf16[48,1664]{1,0:T(8,128)(2,1)} %copy-done.7, bf16[48,1664]{1,0:T(8,128)(2,1)} %copy-done.13, bf16[48,1664]{1,0:T(8,128)(2,1)} %copy-done.6, bf16[48,1664]{1,0:T(8,128)(2,1)} %copy-done.11, ...), custom_call_target="tpu_custom_call" | custom-call | tf_op jit(solution)/shard_map/assemble/pallas_call | solution.py:166
  60.1 5.2 %collective-permute-done.13.other = bf16[8,48,3328]{2,1,0:T(8,128)(2,1)} collective-permute-done((bf16[8,48,3328]{2,1,0:T(8,128)(2,1)}, bf16[8,48,3328]{2,1,0:T(8,128)(2,1)}, u32[]{:S(2)}, u32[]{:S(2)}) %collective-permute-start.13) | collective-permute-done | bytes 2555936 | tf_op jit(solution)/shard_map/ppermute | solution.py:718
  65.3 26.3 %attn_fwd.1 = (bf16[2048,2304]{1,0:T(8,128)(2,1)}, bf16[32,6,64,128]{3,2,1,0:T(8,128)(2,1)}, bf16[2048,768]{1,0:T(8,128)(2,1)}, f32[2048,768]{1,0:T(8,128)}, bf1...) custom-call(s32[32]{0:T(128)} %counts.3, ...), custom_call_target="tpu_custom_call" | custom-call | flops 14495514624 | bytes 31457280 | tf_op jit(solution)/shard_map/attn_fwd/pallas_call | solution.py:249
  93.2 8.5 %all-gather.2.cloned.1.call-done.up = bf16[768,6144]{1,0:T(8,128)(2,1)} async-done(((bf16[48,6144]{1,0:T(8,128)(2,1)}), bf16[768,6144]{1,0:T(8,128)(2,1)}) %all-gather.2.cloned.1.call-update) | async-done | bytes 9437200 | tf_op jit(solution)/shard_map/all_gather | solution.py:768
  101.7 51.9 %mlp.1 = (bf16[2048,3072]{1,0:T(8,128)(2,1)}, bf16[2048,3072]{1,0:T(8,128)(2,1)}, f32[768,128]{1,0:T(8,128)}, bf16[16,48,6144]{2,1,0:T(8,128)(2,1)}) custom-call(bf16[2048,768]{1,0:T(8,128)(2,1)} %get-tuple-element.64.sec_ref, bf16[2048,768]{1,0:T(8,128)(2,1)} %get-tuple-element.65.back_ref, f32[1,3072]{1,0:T(1,128)} %reshape.58.bias_ref, ...), custom_call_target="tpu_custom_call" | custom-call | flops 38654705664 | bytes 18874368 | tf_op jit(solution)/shard_map/mlp/pallas_call | solution.py:348
  153.7 48.1 %attn_bwd.1 = (f32[2048,768]{1,0:T(8,128)}, bf16[2048,2304]{1,0:T(8,128)(2,1)}, bf16[2,4,48,3328]{3,2,1,0:T(8,128)(2,1)}, bf16[2,4,48,3328]{3,2,1,0:T(8,128)(2,1)}) custom-call(bf16[2048,3072]{1,0:T(8,128)(2,1)} %get-tuple-element.69.hg_ref, f32[2048,768]{1,0:T(8,128)} %get-tuple-element.68.mid_ref, bf16[2048,768]{1,0:T(8,128)(2,1)} %get-tuple-element.65.back_ref, ...), custom_call_target="tpu_custom_call" | custom-call | flops 31406948352 | bytes 44040192 | tf_op jit(solution)/shard_map/attn_bwd/pallas_call | solution.py:485
  202.0 4.9 %collective-permute-done.14.got = bf16[2,4,48,3328]{3,2,1,0:T(8,128)(2,1)} collective-permute-done((bf16[2,4,48,3328]{3,2,1,0:T(8,128)(2,1)}, bf16[2,4,48,3328]{3,2,1,0:T(8,128)(2,1)}, u32[]{:S(2)}, u32[]{:S(2)}) %collective-permute-start.14) | collective-permute-done | bytes 2555936 | tf_op jit(solution)/shard_map/ppermute | solution.py:718
  206.9 4.5 %core_sum.1 = (bf16[4,48,1024]{2,1,0:T(8,128)(2,1)}, bf16[4,48,1024]{2,1,0:T(8,128)(2,1)}, bf16[2,4,48,1152]{3,2,1,0:T(8,128)(2,1)}, bf16[2,4,48,1152]{3,2,1,0:T(8,128)(2,1)}) custom-call(bf16[2,4,48,3328]{3,2,1,0:T(8,128)(2,1)} %get-tuple-element.75.near, bf16[2,4,48,3328]{3,2,1,0:T(8,128)(2,1)} %collective-permute-done.14.got), custom_call_target="tpu_custom_call" | custom-call | tf_op jit(solution)/shard_map/core_sum/pallas_call | solution.py:590
  211.5 1.4 collective-permute-start.16
  212.8 16.5 %mixed.1.tie.old = bf16[2048,768]{1,0:T(8,128)(2,1)} custom-call(s32[32]{0:T(128)} %counts.3, bf16[2048,3072]{1,0:T(8,128)(2,1)} %get-tuple-element.67.act_ref, f32[2048,768]{1,0:T(8,128)} %get-tuple-element.68.mid_ref, f32[16,768]{1,0:T(8,128)} %get-tuple-element.66.vec, bf16[16,48,6144]{2,1,0:T(8,128)(2,1)} %bitcast.18, ...), custom_call_target="tpu_custom_call" | custom-call | flops 9663676416 | bytes 22020096 | tf_op jit(solution)/shard_map/mixed/pallas_call | solution.py:552
  229.3 4.2 %collective-permute-done.16.y_got = bf16[2,4,48,1152]{3,2,1,0:T(8,128)(2,1)S(1)} collective-permute-done((bf16[2,4,48,1152]{3,2,1,0:T(8,128)(2,1)}, bf16[2,4,48,1152]{3,2,1,0:T(8,128)(2,1)S(1)}, u32[]{:S(2)}, u32[]{:S(2)}) %collective-permute-start.16) | collective-permute-done | bytes 884768 | tf_op jit(solution)/shard_map/ppermute | solution.py:792
  233.5 0.9 copy-done
  234.4 2.8 across_sum.1
  237.2 1.7 collective-permute-start.18
  238.9 1.4 collective-permute-start.17
  240.3 11.0 %tokens_grad.2.tie.old = bf16[2048,768]{1,0:T(8,128)(2,1)} custom-call(bf16[2048,768]{1,0:T(8,128)(2,1)} %bitcast.12, bf16[2048,2304]{1,0:T(8,128)(2,1)} %get-tuple-element.78.qg_ref, f32[2048,768]{1,0:T(8,128)} %get-tuple-element.79.mg_ref, f32[16,768]{1,0:T(8,128)} %get-tuple-element.66.vec, bf16[8,48,3328]{2,1,0:T(8,128)(2,1)} %assemble.1.mine, ...), custom_call_target="tpu_custom_call" | custom-call | flops 3623878656 | bytes 11010048 | tf_op jit(solution)/shard_map/tokens_grad/pallas_call | solution.py:523
  251.4 2.4 collective-permute-done.18.second_got
  253.8 0.8 copy-done.2
  254.5 2.2 plane_sum.1
  256.7 9.8 %reduce-scatter.2.cloned.1.call-done.a_ref = bf16[48,6144]{1,0:T(8,128)(2,1)} async-done(((bf16[768,6144]{1,0:T(8,128)(2,1)}), bf16[48,6144]{1,0:T(8,128)(2,1)}) %reduce-scatter.2.cloned.1.call-update) | async-done | bytes 589840 | tf_op jit(solution)/shard_map/reduce_scatter | solution.py:784
  266.6 1.5 collective-permute-start.23
  268.0 2.0 collective-permute-start.21
  270.1 2.0 collective-permute-start.19
  272.1 10.8 %tokens_grad.3.tie = bf16[2048,768]{1,0:T(8,128)(2,1)} custom-call(bf16[2048,768]{1,0:T(8,128)(2,1)} %bitcast.13, bf16[2048,2304]{1,0:T(8,128)(2,1)} %get-tuple-element.78.qg_ref, f32[2048,768]{1,0:T(8,128)} %get-tuple-element.79.mg_ref, f32[16,768]{1,0:T(8,128)} %get-tuple-element.66.vec, ...), custom_call_target="tpu_custom_call", output_to_operand_aliasing={{}: (7, {})} | custom-call | flops 3623878656 | bytes 11010048 | tf_op jit(solution)/shard_map/tokens_grad/pallas_call | solution.py:523
  282.9 2.0 collective-permute-done.19.b
  284.9 1.9 along_sum.1.tie.a_ref
  287.3 0.8 copy-done.1
  288.2 2.3 finish_mlp.1
  290.5 1.8 collective-permute-done.22.b_ref
  292.9 1.9 finish.1
  (63 shorter events, 5.6 us)
Async XLA Ops:
  7.2 94.5 %all-gather.2.cloned.1.call-start = ((), (), s32[]{:S(2)}) async-start(), calls=%async_computation.1 | async-start | bytes 10027008 | tf_op jit(solution)/shard_map/all_gather | solution.py:768
  9.2 257.4 %reduce-scatter.2.cloned.1.call-start = ((), (), s32[]{:S(2)}) async-start(), calls=%async_computation.2 | async-start | bytes 10027008 | tf_op jit(solution)/shard_map/reduce_scatter | solution.py:784
  11.3 9.9 %collective-permute-start.5 = (bf16[48,1664]{1,0:T(8,128)(2,1)}, bf16[48,1664]{1,0:T(8,128)(2,1)S(1)}, u32[]{:S(2)}, u32[]{:S(2)}) collective-permute-start(bf16[48,1664]{1,0:T(8,128)(2,1)} %get-tuple-element.63), channel_id=1, source_target_pairs={{0,24},{2,26},{4,28},{6,30},{8,0},{10,2},{12,4},{14,6},{16,8},{18,... | collective-permute-start | bytes 479240 | tf_op jit(solution)/shard_map/ppermute | solution.py:718
  16.3 21.5 %collective-permute-start.3 = (bf16[48,1664]{1,0:T(8,128)(2,1)}, bf16[48,1664]{1,0:T(8,128)(2,1)S(1)}, u32[]{:S(2)}, u32[]{:S(2)}) collective-permute-start(bf16[48,1664]{1,0:T(8,128)(2,1)} %get-tuple-element.63), channel_id=1, source_target_pairs={{0,16},{2,18},{4,20},{6,22},{8,24},{10,26},{12,28},{14,30},{16,0},... | collective-permute-start | bytes 479240 | tf_op jit(solution)/shard_map/ppermute | solution.py:718
  16.3 23.7 %collective-permute-start.1 = (bf16[48,1664]{1,0:T(8,128)(2,1)}, bf16[48,1664]{1,0:T(8,128)(2,1)S(1)}, u32[]{:S(2)}, u32[]{:S(2)}) collective-permute-start(bf16[48,1664]{1,0:T(8,128)(2,1)} %get-tuple-element.63), channel_id=1, source_target_pairs={{0,8},{2,10},{4,12},{6,14},{8,16},{10,18},{12,20},{14,22},{16,24},... | collective-permute-start | bytes 479240 | tf_op jit(solution)/shard_map/ppermute | solution.py:718
  21.2 35.4 %copy-start.5 = (bf16[48,1664]{1,0:T(8,128)(2,1)}, bf16[48,1664]{1,0:T(8,128)(2,1)S(1)}, u32[]{:S(2)}) copy-start(bf16[48,1664]{1,0:T(8,128)(2,1)S(1)} %collective-permute-done.5.refs_4_) | copy-start | bytes 479236
  21.2 20.4 %collective-permute-start.11 = (bf16[48,1664]{1,0:T(8,128)(2,1)S(1)}, bf16[48,1664]{1,0:T(8,128)(2,1)S(1)}, u32[]{:S(2)}, u32[]{:S(2)}) collective-permute-start(bf16[48,1664]{1,0:T(8,128)(2,1)S(1)} %collective-permute-done.5.refs_4_), channel_id=1, source_target_pairs={{0,4},{2,6},{4,0},{6,2},{8,12},{10,14},{12,8},{14,10},{16,20},{18,... | collective-permute-start | bytes 479240 | tf_op jit(solution)/shard_map/ppermute | solution.py:718
  22.7 27.7 %collective-permute-start = (bf16[48,3328]{1,0:T(8,128)(2,1)}, bf16[48,3328]{1,0:T(8,128)(2,1)S(1)}, u32[]{:S(2)}, u32[]{:S(2)}) collective-permute-start(bf16[48,3328]{1,0:T(8,128)(2,1)} %get-tuple-element.62.own), channel_id=1, source_target_pairs={{0,4},{2,6},{4,0},{6,2},{8,12},{10,14},{12,8},{14,10},{16,20},{18,... | collective-permute-start | bytes 958472 | tf_op jit(solution)/shard_map/ppermute | solution.py:718
  23.2 18.4 %collective-permute-start.6 = (bf16[48,1664]{1,0:T(8,128)(2,1)S(1)}, bf16[48,1664]{1,0:T(8,128)(2,1)S(1)}, u32[]{:S(2)}, u32[]{:S(2)}) collective-permute-start(bf16[48,1664]{1,0:T(8,128)(2,1)S(1)} %collective-permute-done.5.refs_4_), channel_id=1, source_target_pairs={{0,1},{1,0},{2,3},{3,2},{4,5},{5,4},{6,7},{7,6},{8,9},{9,8},{10,11... | collective-permute-start | bytes 479240 | tf_op jit(solution)/shard_map/ppermute | solution.py:722
  37.8 18.7 %copy-start.6 = (bf16[48,1664]{1,0:T(8,128)(2,1)}, bf16[48,1664]{1,0:T(8,128)(2,1)S(1)}, u32[]{:S(2)}) copy-start(bf16[48,1664]{1,0:T(8,128)(2,1)S(1)} %collective-permute-done.3.refs_2_) | copy-start | bytes 479236
  37.8 6.1 %collective-permute-start.9 = (bf16[48,1664]{1,0:T(8,128)(2,1)S(1)}, bf16[48,1664]{1,0:T(8,128)(2,1)S(1)}, u32[]{:S(2)}, u32[]{:S(2)}) collective-permute-start(bf16[48,1664]{1,0:T(8,128)(2,1)S(1)} %collective-permute-done.3.refs_2_), channel_id=1, source_target_pairs={{0,4},{2,6},{4,0},{6,2},{8,12},{10,14},{12,8},{14,10},{16,20},{18,... | collective-permute-start | bytes 479240 | tf_op jit(solution)/shard_map/ppermute | solution.py:718
  40.0 16.5 %copy-start.7 = (bf16[48,1664]{1,0:T(8,128)(2,1)}, bf16[48,1664]{1,0:T(8,128)(2,1)S(1)}, u32[]{:S(2)}) copy-start(bf16[48,1664]{1,0:T(8,128)(2,1)S(1)} %collective-permute-done.1.refs_0_) | copy-start | bytes 479236
  40.0 7.0 %collective-permute-start.4 = (bf16[48,1664]{1,0:T(8,128)(2,1)S(1)}, bf16[48,1664]{1,0:T(8,128)(2,1)S(1)}, u32[]{:S(2)}, u32[]{:S(2)}) collective-permute-start(bf16[48,1664]{1,0:T(8,128)(2,1)S(1)} %collective-permute-done.3.refs_2_), channel_id=1, source_target_pairs={{0,1},{1,0},{2,3},{3,2},{4,5},{5,4},{6,7},{7,6},{8,9},{9,8},{10,11... | collective-permute-start | bytes 479240 | tf_op jit(solution)/shard_map/ppermute | solution.py:722
  41.5 15.0 %copy-start.8 = (bf16[48,1664]{1,0:T(8,128)(2,1)}, bf16[48,1664]{1,0:T(8,128)(2,1)S(1)}, u32[]{:S(2)}) copy-start(bf16[48,1664]{1,0:T(8,128)(2,1)S(1)} %collective-permute-done.11.refs_10_) | copy-start | bytes 479236
  41.5 7.0 %collective-permute-start.7 = (bf16[48,1664]{1,0:T(8,128)(2,1)S(1)}, bf16[48,1664]{1,0:T(8,128)(2,1)S(1)}, u32[]{:S(2)}, u32[]{:S(2)}) collective-permute-start(bf16[48,1664]{1,0:T(8,128)(2,1)S(1)} %collective-permute-done.1.refs_0_), channel_id=1, source_target_pairs={{0,4},{2,6},{4,0},{6,2},{8,12},{10,14},{12,8},{14,10},{16,20},{18,... | collective-permute-start | bytes 479240 | tf_op jit(solution)/shard_map/ppermute | solution.py:718
  41.6 11.4 %copy-start.9 = (bf16[48,1664]{1,0:T(8,128)(2,1)}, bf16[48,1664]{1,0:T(8,128)(2,1)S(1)}, u32[]{:S(2)}) copy-start(bf16[48,1664]{1,0:T(8,128)(2,1)S(1)} %collective-permute-done.6.refs_5_) | copy-start | bytes 479236
  41.6 8.8 %collective-permute-start.2 = (bf16[48,1664]{1,0:T(8,128)(2,1)S(1)}, bf16[48,1664]{1,0:T(8,128)(2,1)S(1)}, u32[]{:S(2)}, u32[]{:S(2)}) collective-permute-start(bf16[48,1664]{1,0:T(8,128)(2,1)S(1)} %collective-permute-done.1.refs_0_), channel_id=1, source_target_pairs={{0,1},{1,0},{2,3},{3,2},{4,5},{5,4},{6,7},{7,6},{8,9},{9,8},{10,11... | collective-permute-start | bytes 479240 | tf_op jit(solution)/shard_map/ppermute | solution.py:722
  43.9 10.9 %copy-start.10 = (bf16[48,1664]{1,0:T(8,128)(2,1)}, bf16[48,1664]{1,0:T(8,128)(2,1)S(1)}, u32[]{:S(2)}) copy-start(bf16[48,1664]{1,0:T(8,128)(2,1)S(1)} %collective-permute-done.9.refs_8_) | copy-start | bytes 479236
  43.9 9.1 %collective-permute-start.12 = (bf16[48,1664]{1,0:T(8,128)(2,1)S(1)}, bf16[48,1664]{1,0:T(8,128)(2,1)S(1)}, u32[]{:S(2)}, u32[]{:S(2)}) collective-permute-start(bf16[48,1664]{1,0:T(8,128)(2,1)S(1)} %collective-permute-done.11.refs_10_), channel_id=1, source_target_pairs={{0,1},{1,0},{2,3},{3,2},{4,5},{5,4},{6,7},{7,6},{8,9},{9,8},{10,11... | collective-permute-start | bytes 479240 | tf_op jit(solution)/shard_map/ppermute | solution.py:722
  47.0 7.8 %copy-start.11 = (bf16[48,1664]{1,0:T(8,128)(2,1)}, bf16[48,1664]{1,0:T(8,128)(2,1)S(1)}, u32[]{:S(2)}) copy-start(bf16[48,1664]{1,0:T(8,128)(2,1)S(1)} %collective-permute-done.4.refs_3_) | copy-start | bytes 479236
  47.0 7.8 %collective-permute-start.10 = (bf16[48,1664]{1,0:T(8,128)(2,1)S(1)}, bf16[48,1664]{1,0:T(8,128)(2,1)S(1)}, u32[]{:S(2)}, u32[]{:S(2)}) collective-permute-start(bf16[48,1664]{1,0:T(8,128)(2,1)S(1)} %collective-permute-done.9.refs_8_), channel_id=1, source_target_pairs={{0,1},{1,0},{2,3},{3,2},{4,5},{5,4},{6,7},{7,6},{8,9},{9,8},{10,11... | collective-permute-start | bytes 479240 | tf_op jit(solution)/shard_map/ppermute | solution.py:722
  48.5 6.2 %copy-start.12 = (bf16[48,1664]{1,0:T(8,128)(2,1)}, bf16[48,1664]{1,0:T(8,128)(2,1)S(1)}, u32[]{:S(2)}) copy-start(bf16[48,1664]{1,0:T(8,128)(2,1)S(1)} %collective-permute-done.7.refs_6_) | copy-start | bytes 479236
  48.5 8.0 %collective-permute-start.8 = (bf16[48,1664]{1,0:T(8,128)(2,1)S(1)}, bf16[48,1664]{1,0:T(8,128)(2,1)}, u32[]{:S(2)}, u32[]{:S(2)}) collective-permute-start(bf16[48,1664]{1,0:T(8,128)(2,1)S(1)} %collective-permute-done.7.refs_6_), channel_id=1, source_target_pairs={{0,1},{1,0},{2,3},{3,2},{4,5},{5,4},{6,7},{7,6},{8,9},{9,8},{10,11... | collective-permute-start | bytes 479240 | tf_op jit(solution)/shard_map/ppermute | solution.py:722
  50.4 4.4 %copy-start.13 = (bf16[48,1664]{1,0:T(8,128)(2,1)}, bf16[48,1664]{1,0:T(8,128)(2,1)S(1)}, u32[]{:S(2)}) copy-start(bf16[48,1664]{1,0:T(8,128)(2,1)S(1)} %collective-permute-done.2.refs_1_) | copy-start | bytes 479236
  50.4 6.2 %copy-start.3 = (bf16[48,3328]{1,0:T(8,128)(2,1)}, bf16[48,3328]{1,0:T(8,128)(2,1)S(1)}, u32[]{:S(2)}) copy-start(bf16[48,3328]{1,0:T(8,128)(2,1)S(1)} %collective-permute-done.across) | copy-start | bytes 958468
  53.0 1.7 copy-start.14
  54.8 0.7 copy-start.15
  60.1 5.2 %collective-permute-start.13 = (bf16[8,48,3328]{2,1,0:T(8,128)(2,1)}, bf16[8,48,3328]{2,1,0:T(8,128)(2,1)}, u32[]{:S(2)}, u32[]{:S(2)}) collective-permute-start(bf16[8,48,3328]{2,1,0:T(8,128)(2,1)} %assemble.1.mine), channel_id=1, source_target_pairs={{0,2},{2,0},{4,6},{6,4},{8,10},{10,8},{12,14},{14,12},{16,18},{18,... | collective-permute-start | bytes 7667720 | tf_op jit(solution)/shard_map/ppermute | solution.py:718
  201.7 5.2 %collective-permute-start.14 = (bf16[2,4,48,3328]{3,2,1,0:T(8,128)(2,1)}, bf16[2,4,48,3328]{3,2,1,0:T(8,128)(2,1)}, u32[]{:S(2)}, u32[]{:S(2)}) collective-permute-start(bf16[2,4,48,3328]{3,2,1,0:T(8,128)(2,1)} %get-tuple-element.76), channel_id=1, source_target_pairs={{0,2},{2,0},{4,6},{6,4},{8,10},{10,8},{12,14},{14,12},{16,18},{18,... | collective-permute-start | bytes 7667720 | tf_op jit(solution)/shard_map/ppermute | solution.py:718
  211.5 17.9 %collective-permute-start.15 = (bf16[4,48,1024]{2,1,0:T(8,128)(2,1)}, bf16[4,48,1024]{2,1,0:T(8,128)(2,1)}, u32[]{:S(2)}, u32[]{:S(2)}) collective-permute-start(bf16[4,48,1024]{2,1,0:T(8,128)(2,1)} %get-tuple-element.77.tie.old), channel_id=1, source_target_pairs={{0,4},{2,6},{4,0},{6,2},{8,12},{10,14},{12,8},{14,10},{16,20},{18,... | collective-permute-start | bytes 1179656 | tf_op jit(solution)/shard_map/ppermute | solution.py:718
  211.5 22.1 %collective-permute-start.16 = (bf16[2,4,48,1152]{3,2,1,0:T(8,128)(2,1)}, bf16[2,4,48,1152]{3,2,1,0:T(8,128)(2,1)S(1)}, u32[]{:S(2)}, u32[]{:S(2)}) collective-permute-start(bf16[2,4,48,1152]{3,2,1,0:T(8,128)(2,1)} %get-tuple-element.82), channel_id=1, source_target_pairs={{0,1},{1,0},{2,3},{3,2},{4,5},{5,4},{6,7},{7,6},{8,9},{9,8},{10,11... | collective-permute-start | bytes 2654216 | tf_op jit(solution)/shard_map/ppermute | solution.py:792
  233.5 0.9 copy-start
  237.2 16.5 %collective-permute-start.18 = (bf16[4,48,1152]{2,1,0:T(8,128)(2,1)}, bf16[4,48,1152]{2,1,0:T(8,128)(2,1)S(1)}, u32[]{:S(2)}, u32[]{:S(2)}) collective-permute-start(bf16[4,48,1152]{2,1,0:T(8,128)(2,1)} %get-tuple-element.86), channel_id=1, source_target_pairs={{0,4},{2,6},{4,0},{6,2},{8,12},{10,14},{12,8},{14,10},{16,20},{18,... | collective-permute-start | bytes 1327112 | tf_op jit(solution)/shard_map/ppermute | solution.py:718
  238.9 12.4 %collective-permute-start.17 = (bf16[4,48,512]{2,1,0:T(8,128)(2,1)}, bf16[4,48,512]{2,1,0:T(8,128)(2,1)S(1)}, u32[]{:S(2)}, u32[]{:S(2)}) collective-permute-start(bf16[4,48,512]{2,1,0:T(8,128)(2,1)} %get-tuple-element.84.tie), channel_id=1, source_target_pairs={{0,1},{1,0},{2,3},{3,2},{4,5},{5,4},{6,7},{7,6},{8,9},{9,8},{10,11... | collective-permute-start | bytes 589832 | tf_op jit(solution)/shard_map/ppermute | solution.py:795
  251.3 2.4 copy-start.4
  253.7 0.8 copy-start.2
  266.6 20.8 %collective-permute-start.23 = (bf16[48,6144]{1,0:T(8,128)(2,1)}, bf16[48,6144]{1,0:T(8,128)(2,1)S(1)}, u32[]{:S(2)}, u32[]{:S(2)}) collective-permute-start(bf16[48,6144]{1,0:T(8,128)(2,1)} %reduce-scatter.2.cloned.1.call-done.a_ref), channel_id=1, source_target_pairs={{0,1},{1,0},{2,3},{3,2},{4,5},{5,4},{6,7},{7,6},{8,9},{9,8},{10,11... | collective-permute-start | bytes 1769480 | tf_op jit(solution)/shard_map/ppermute | solution.py:801
  268.0 14.8 %collective-permute-start.21 = (bf16[48,1664]{1,0:T(8,128)(2,1)}, bf16[48,1664]{1,0:T(8,128)(2,1)S(1)}, u32[]{:S(2)}, u32[]{:S(2)}) collective-permute-start(bf16[48,1664]{1,0:T(8,128)(2,1)} %get-tuple-element.94.tie), channel_id=1, source_target_pairs={{0,24},{2,26},{4,28},{6,30},{8,0},{10,2},{12,4},{14,6},{16,8},{18,... | collective-permute-start | bytes 479240 | tf_op jit(solution)/shard_map/ppermute | solution.py:718
  270.0 12.9 %collective-permute-start.20 = (bf16[48,1664]{1,0:T(8,128)(2,1)}, bf16[48,1664]{1,0:T(8,128)(2,1)S(1)}, u32[]{:S(2)}, u32[]{:S(2)}) collective-permute-start(bf16[48,1664]{1,0:T(8,128)(2,1)} %get-tuple-element.93), channel_id=1, source_target_pairs={{0,8},{2,10},{4,12},{6,14},{8,16},{10,18},{12,20},{14,22},{16,24},... | collective-permute-start | bytes 479240 | tf_op jit(solution)/shard_map/ppermute | solution.py:718
  270.1 14.8 %collective-permute-start.19 = (bf16[48,1664]{1,0:T(8,128)(2,1)}, bf16[48,1664]{1,0:T(8,128)(2,1)}, u32[]{:S(2)}, u32[]{:S(2)}) collective-permute-start(bf16[48,1664]{1,0:T(8,128)(2,1)} %get-tuple-element.91), channel_id=1, source_target_pairs={{0,16},{2,18},{4,20},{6,22},{8,24},{10,26},{12,28},{14,30},{16,0},... | collective-permute-start | bytes 479240 | tf_op jit(solution)/shard_map/ppermute | solution.py:718
  282.9 2.0 copy-start.16
  282.9 2.0 copy-start.17
  286.8 5.5 %collective-permute-start.22 = (bf16[48,1664]{1,0:T(8,128)(2,1)}, bf16[48,1664]{1,0:T(8,128)(2,1)S(1)}, u32[]{:S(2)}, u32[]{:S(2)}) collective-permute-start(bf16[48,1664]{1,0:T(8,128)(2,1)} %along_sum.1.tie.a_ref), channel_id=1, source_target_pairs={{0,1},{1,0},{2,3},{3,2},{4,5},{5,4},{6,7},{7,6},{8,9},{9,8},{10,11... | collective-permute-start | bytes 479240 | tf_op jit(solution)/shard_map/ppermute | solution.py:804
  287.3 0.8 copy-start.1
  292.3 0.7 copy-start.18
Sparse Core Ops, SparseCore 0:
  10.9 90.8 all-gather.1
  153.8 112.7 reduce-scatter.1
where the time goes:
time: 303 us; the launch traced here: 302 us
  Pallas kernels  188 us (62%)
  waiting for transfers between devices  66.5 us (22%)
  starting transfers between devices  27.8 us (9%)
  between operations  14.3 us (5%)
  local copies, waits for them, and re-layouts  5.44 us (2%)
    pallas_call x1, Pallas kernels, mlp(): pl.pallas_call(functools.partial(mlp_kernel, chunk), grid=(ff // f,), in_...  51.9 us
    pallas_call x1, Pallas kernels, attn_bwd(): pl.pallas_call(functools.partial(attn_bwd_kernel, hier), grid=(steps + 1,...  48.1 us
    ppermute x14, waiting for transfers between devices, permute(): return lax.ppermute(v, 'fsdp', pairs)  33.2 us
    pallas_call x1, Pallas kernels, attn_fwd(): pl.pallas_call(functools.partial(attn_fwd_kernel, chunk, hier), grid=(tot...  26.3 us
    pallas_call x2, Pallas kernels, tokens_grad(): pl.pallas_call(functools.partial(tokens_grad_kernel, hier), grid=(blocks,...  21.8 us
    pallas_call x1, Pallas kernels, mixed_out(): pl.pallas_call(functools.partial(mixed_kernel, first), grid=(blocks,), in...  16.5 us
    ppermute x14, starting transfers between devices, permute(): return lax.ppermute(v, 'fsdp', pairs)  16.4 us
    reduce_scatter x1, waiting for transfers between devices, local(): lax.psum_scatter(grads.reshape(width, 2 * ff), 'fsdp', scatter_dimension=...  9.83 us
  transfers between devices with their start and end apart: 26, of which 16 were waited for; matrix products, arithmetic and copies ran while one was open for 1% of the time, Pallas kernels for 44%

commit v1 on v0

--- a/solution.py
+++ b/solution.py
@@ -793,10 +793,10 @@
         mixed = mix(x_send)
         first_keep, first_send, second_keep, second_send = across_sum(x_keep, x_got, y_keep, y_got, mixed)
         first_got, second_got = lax.ppermute(first_send, "rep", SWAP), permute(second_send, ACROSS)
-        toks = tok(0, blocks // 2, first_send, mixed)
+        toks = tok(0, 5 * blocks // 8, first_send, mixed)
         parts = plane_sum(first_keep, first_got, second_keep, second_got, toks)
-        moved = [permute(after(parts[k], mlp_grads), ALONG[k]) for k in (2, 1, 3)]
-        toks = tok(blocks // 2, blocks, parts[3], toks)
+        moved = [permute(parts[k] if k == 2 else after(parts[k], mlp_grads), ALONG[k]) for k in (2, 1, 3)]
+        toks = tok(5 * blocks // 8, blocks, parts[3], toks)
         mlp_grads = after(mlp_grads, parts[3])
         mlp_got = lax.ppermute(mlp_grads, "rep", SWAP)
         low = along_sum(parts[0], *moved, toks)

time: 303 us -> 301 us (level)
  no operation moved by 1% of the time
where the time goes in v1:
time: 301 us; the launch traced here: 300 us
  Pallas kernels  188 us (62%)
  waiting for transfers between devices  63.9 us (21%)
  starting transfers between devices  27.8 us (9%)
  between operations  14.2 us (5%)
  local copies, waits for them, and re-layouts  6.13 us (2%)
    pallas_call x1, Pallas kernels, mlp(): pl.pallas_call(functools.partial(mlp_kernel, chunk), grid=(ff // f,), in_...  51.9 us
    pallas_call x1, Pallas kernels, attn_bwd(): pl.pallas_call(functools.partial(attn_bwd_kernel, hier), grid=(steps + 1,...  48.1 us
    ppermute x14, waiting for transfers between devices, permute(): return lax.ppermute(v, 'fsdp', pairs)  30.5 us
    pallas_call x1, Pallas kernels, attn_fwd(): pl.pallas_call(functools.partial(attn_fwd_kernel, chunk, hier), grid=(tot...  26.3 us
    pallas_call x2, Pallas kernels, tokens_grad(): pl.pallas_call(functools.partial(tokens_grad_kernel, hier), grid=(blocks,...  22 us
    pallas_call x1, Pallas kernels, mixed_out(): pl.pallas_call(functools.partial(mixed_kernel, first), grid=(blocks,), in...  16.5 us
    ppermute x14, starting transfers between devices, permute(): return lax.ppermute(v, 'fsdp', pairs)  16.4 us
    reduce_scatter x1, waiting for transfers between devices, local(): lax.psum_scatter(grads.reshape(width, 2 * ff), 'fsdp', scatter_dimension=...  9.83 us
  transfers between devices with their start and end apart: 26, of which 16 were waited for; matrix products, arithmetic and copies ran while one was open for 1% of the time, Pallas kernels for 44%

profile of v1, /device:TPU:0, one launch (start us, length us, event | category | flops | bytes accessed | tf_op | source)
XLA Modules:
  0.0 300.0 jit_solution(4762482712056584208)
XLA Ops:
  7.2 1.9 pack_mlp.1
  9.2 2.0 pack.1
  11.3 5.0 %collective-permute-start.5 = (bf16[48,1664]{1,0:T(8,128)(2,1)}, bf16[48,1664]{1,0:T(8,128)(2,1)S(1)}, u32[]{:S(2)}, u32[]{:S(2)}) collective-permute-start(bf16[48,1664]{1,0:T(8,128)(2,1)} %get-tuple-element.62), channel_id=1, source_target_pairs={{0,24},{2,26},{4,28},{6,30},{8,0},{10,2},{12,4},{14,6},{16,8},{18,... | collective-permute-start | bytes 479240 | tf_op jit(solution)/shard_map/ppermute | solution.py:718
  16.3 1.0 collective-permute-start.1
  17.3 3.9 %collective-permute-done.5.refs_4_ = bf16[48,1664]{1,0:T(8,128)(2,1)S(1)} collective-permute-done((bf16[48,1664]{1,0:T(8,128)(2,1)}, bf16[48,1664]{1,0:T(8,128)(2,1)S(1)}, u32[]{:S(2)}, u32[]{:S(2)}) %collective-permute-start.5) | collective-permute-done | bytes 159776 | tf_op jit(solution)/shard_map/ppermute | solution.py:718
  21.2 1.5 collective-permute-start.11
  23.2 1.5 collective-permute-start.6
  24.7 13.1 %collective-permute-done.3.refs_2_ = bf16[48,1664]{1,0:T(8,128)(2,1)S(1)} collective-permute-done((bf16[48,1664]{1,0:T(8,128)(2,1)}, bf16[48,1664]{1,0:T(8,128)(2,1)S(1)}, u32[]{:S(2)}, u32[]{:S(2)}) %collective-permute-start.3) | collective-permute-done | bytes 159776 | tf_op jit(solution)/shard_map/ppermute | solution.py:718
  37.8 2.2 collective-permute-start.9
  40.0 1.5 collective-permute-start.4
  42.1 1.7 collective-permute-done.9.refs_8_
  43.9 1.0 collective-permute-start.12
  44.9 2.1 collective-permute-done.4.refs_3_
  47.0 1.5 collective-permute-start.10
  49.0 1.4 collective-permute-done.2.refs_1_
  50.4 2.6 collective-permute-done.12.refs_11_
  53.0 1.7 collective-permute-done.10.refs_9_
  55.4 1.1 collective-permute-done.8.refs_7_
  56.6 3.5 %assemble.1.mine = bf16[8,48,3328]{2,1,0:T(8,128)(2,1)} custom-call(bf16[48,3328]{1,0:T(8,128)(2,1)} %get-tuple-element.61.own, bf16[48,3328]{1,0:T(8,128)(2,1)} %copy-done.3, bf16[48,1664]{1,0:T(8,128)(2,1)} %copy-done.7, bf16[48,1664]{1,0:T(8,128)(2,1)} %copy-done.13, bf16[48,1664]{1,0:T(8,128)(2,1)} %copy-done.6, bf16[48,1664]{1,0:T(8,128)(2,1)} %copy-done.11, ...), custom_call_target="tpu_custom_call" | custom-call | tf_op jit(solution)/shard_map/assemble/pallas_call | solution.py:166
  60.1 5.2 %collective-permute-done.13.other = bf16[8,48,3328]{2,1,0:T(8,128)(2,1)} collective-permute-done((bf16[8,48,3328]{2,1,0:T(8,128)(2,1)}, bf16[8,48,3328]{2,1,0:T(8,128)(2,1)}, u32[]{:S(2)}, u32[]{:S(2)}) %collective-permute-start.13) | collective-permute-done | bytes 2555936 | tf_op jit(solution)/shard_map/ppermute | solution.py:718
  65.3 26.3 %attn_fwd.1 = (bf16[2048,2304]{1,0:T(8,128)(2,1)}, bf16[32,6,64,128]{3,2,1,0:T(8,128)(2,1)}, bf16[2048,768]{1,0:T(8,128)(2,1)}, f32[2048,768]{1,0:T(8,128)}, bf1...) custom-call(s32[32]{0:T(128)} %counts.3, ...), custom_call_target="tpu_custom_call" | custom-call | flops 14495514624 | bytes 31457280 | tf_op jit(solution)/shard_map/attn_fwd/pallas_call | solution.py:249
  91.6 0.7 slice.3
  93.2 8.5 %all-gather.2.cloned.1.call-done.up = bf16[768,6144]{1,0:T(8,128)(2,1)} async-done(((bf16[48,6144]{1,0:T(8,128)(2,1)}), bf16[768,6144]{1,0:T(8,128)(2,1)}) %all-gather.2.cloned.1.call-update) | async-done | bytes 9437200 | tf_op jit(solution)/shard_map/all_gather | solution.py:768
  101.7 51.9 %mlp.1 = (bf16[2048,3072]{1,0:T(8,128)(2,1)}, bf16[2048,3072]{1,0:T(8,128)(2,1)}, f32[768,128]{1,0:T(8,128)}, bf16[16,48,6144]{2,1,0:T(8,128)(2,1)}) custom-call(bf16[2048,768]{1,0:T(8,128)(2,1)} %get-tuple-element.63.sec_ref, bf16[2048,768]{1,0:T(8,128)(2,1)} %get-tuple-element.64.back_ref, f32[1,3072]{1,0:T(1,128)} %reshape.58.bias_ref, ...), custom_call_target="tpu_custom_call" | custom-call | flops 38654705664 | bytes 18874368 | tf_op jit(solution)/shard_map/mlp/pallas_call | solution.py:348
  153.7 48.1 %attn_bwd.1 = (f32[2048,768]{1,0:T(8,128)}, bf16[2048,2304]{1,0:T(8,128)(2,1)}, bf16[2,4,48,3328]{3,2,1,0:T(8,128)(2,1)}, bf16[2,4,48,3328]{3,2,1,0:T(8,128)(2,1)}) custom-call(bf16[2048,3072]{1,0:T(8,128)(2,1)} %get-tuple-element.68.hg_ref, f32[2048,768]{1,0:T(8,128)} %get-tuple-element.67.mid_ref, bf16[2048,768]{1,0:T(8,128)(2,1)} %get-tuple-element.64.back_ref, ...), custom_call_target="tpu_custom_call" | custom-call | flops 31406948352 | bytes 44040192 | tf_op jit(solution)/shard_map/attn_bwd/pallas_call | solution.py:485
  202.0 4.9 %collective-permute-done.14.got = bf16[2,4,48,3328]{3,2,1,0:T(8,128)(2,1)} collective-permute-done((bf16[2,4,48,3328]{3,2,1,0:T(8,128)(2,1)}, bf16[2,4,48,3328]{3,2,1,0:T(8,128)(2,1)}, u32[]{:S(2)}, u32[]{:S(2)}) %collective-permute-start.14) | collective-permute-done | bytes 2555936 | tf_op jit(solution)/shard_map/ppermute | solution.py:718
  206.9 4.5 %core_sum.1 = (bf16[4,48,1024]{2,1,0:T(8,128)(2,1)}, bf16[4,48,1024]{2,1,0:T(8,128)(2,1)}, bf16[2,4,48,1152]{3,2,1,0:T(8,128)(2,1)}, bf16[2,4,48,1152]{3,2,1,0:T(8,128)(2,1)}) custom-call(bf16[2,4,48,3328]{3,2,1,0:T(8,128)(2,1)} %get-tuple-element.74.near, bf16[2,4,48,3328]{3,2,1,0:T(8,128)(2,1)} %collective-permute-done.14.got), custom_call_target="tpu_custom_call" | custom-call | tf_op jit(solution)/shard_map/core_sum/pallas_call | solution.py:590
  211.5 1.4 collective-permute-start.16
  212.8 16.5 %mixed.1.tie.old = bf16[2048,768]{1,0:T(8,128)(2,1)} custom-call(s32[32]{0:T(128)} %counts.3, bf16[2048,3072]{1,0:T(8,128)(2,1)} %get-tuple-element.66.act_ref, f32[2048,768]{1,0:T(8,128)} %get-tuple-element.67.mid_ref, f32[16,768]{1,0:T(8,128)} %get-tuple-element.65.vec, bf16[16,48,6144]{2,1,0:T(8,128)(2,1)} %bitcast.18, ...), custom_call_target="tpu_custom_call" | custom-call | flops 9663676416 | bytes 22020096 | tf_op jit(solution)/shard_map/mixed/pallas_call | solution.py:552
  229.3 4.2 %collective-permute-done.16.y_got = bf16[2,4,48,1152]{3,2,1,0:T(8,128)(2,1)S(1)} collective-permute-done((bf16[2,4,48,1152]{3,2,1,0:T(8,128)(2,1)}, bf16[2,4,48,1152]{3,2,1,0:T(8,128)(2,1)S(1)}, u32[]{:S(2)}, u32[]{:S(2)}) %collective-permute-start.16) | collective-permute-done | bytes 884768 | tf_op jit(solution)/shard_map/ppermute | solution.py:792
  233.5 0.9 copy-done
  234.4 2.8 across_sum.1
  237.2 1.7 collective-permute-start.18
  238.9 1.4 collective-permute-start.17
  240.3 12.7 %tokens_grad.2.tie.old = bf16[2048,768]{1,0:T(8,128)(2,1)} custom-call(bf16[2048,768]{1,0:T(8,128)(2,1)} %bitcast.12, bf16[2048,2304]{1,0:T(8,128)(2,1)} %get-tuple-element.77.qg_ref, f32[2048,768]{1,0:T(8,128)} %get-tuple-element.78.mg_ref, f32[16,768]{1,0:T(8,128)} %get-tuple-element.65.vec, bf16[8,48,3328]{2,1,0:T(8,128)(2,1)} %assemble.1.mine, ...), custom_call_target="tpu_custom_call" | custom-call | flops 4529848320 | bytes 13762560 | tf_op jit(solution)/shard_map/tokens_grad/pallas_call | solution.py:523
  253.8 0.8 copy-done.2
  254.5 2.2 plane_sum.1
  256.7 9.8 %reduce-scatter.2.cloned.1.call-done.a_ref = bf16[48,6144]{1,0:T(8,128)(2,1)} async-done(((bf16[768,6144]{1,0:T(8,128)(2,1)}), bf16[48,6144]{1,0:T(8,128)(2,1)}) %reduce-scatter.2.cloned.1.call-update) | async-done | bytes 589840 | tf_op jit(solution)/shard_map/reduce_scatter | solution.py:784
  266.6 1.5 collective-permute-start.23
  268.0 2.0 collective-permute-start.19
  270.0 1.8 collective-permute-start.21
  272.1 9.3 %tokens_grad.3.tie = bf16[2048,768]{1,0:T(8,128)(2,1)} custom-call(bf16[2048,768]{1,0:T(8,128)(2,1)} %bitcast.13, bf16[2048,2304]{1,0:T(8,128)(2,1)} %get-tuple-element.77.qg_ref, f32[2048,768]{1,0:T(8,128)} %get-tuple-element.78.mg_ref, f32[16,768]{1,0:T(8,128)} %get-tuple-element.65.vec, ...), custom_call_target="tpu_custom_call", output_to_operand_aliasing={{}: (7, {})} | custom-call | flops 2717908992 | bytes 8257536 | tf_op jit(solution)/shard_map/tokens_grad/pallas_call | solution.py:523
  281.4 1.0 collective-permute-done.19.b
  283.1 1.9 along_sum.1.tie.a_ref
  285.6 0.8 copy-done.1
  286.4 2.3 finish_mlp.1
  288.7 1.8 collective-permute-done.22.b_ref
  291.2 1.9 finish.1
  (63 shorter events, 6.5 us)
Async XLA Ops:
  7.2 94.5 %all-gather.2.cloned.1.call-start = ((), (), s32[]{:S(2)}) async-start(), calls=%async_computation.1 | async-start | bytes 10027008 | tf_op jit(solution)/shard_map/all_gather | solution.py:768
  9.2 257.4 %reduce-scatter.2.cloned.1.call-start = ((), (), s32[]{:S(2)}) async-start(), calls=%async_computation.2 | async-start | bytes 10027008 | tf_op jit(solution)/shard_map/reduce_scatter | solution.py:784
  11.3 9.9 %collective-permute-start.5 = (bf16[48,1664]{1,0:T(8,128)(2,1)}, bf16[48,1664]{1,0:T(8,128)(2,1)S(1)}, u32[]{:S(2)}, u32[]{:S(2)}) collective-permute-start(bf16[48,1664]{1,0:T(8,128)(2,1)} %get-tuple-element.62), channel_id=1, source_target_pairs={{0,24},{2,26},{4,28},{6,30},{8,0},{10,2},{12,4},{14,6},{16,8},{18,... | collective-permute-start | bytes 479240 | tf_op jit(solution)/shard_map/ppermute | solution.py:718
  16.3 21.5 %collective-permute-start.3 = (bf16[48,1664]{1,0:T(8,128)(2,1)}, bf16[48,1664]{1,0:T(8,128)(2,1)S(1)}, u32[]{:S(2)}, u32[]{:S(2)}) collective-permute-start(bf16[48,1664]{1,0:T(8,128)(2,1)} %get-tuple-element.62), channel_id=1, source_target_pairs={{0,16},{2,18},{4,20},{6,22},{8,24},{10,26},{12,28},{14,30},{16,0},... | collective-permute-start | bytes 479240 | tf_op jit(solution)/shard_map/ppermute | solution.py:718
  16.3 23.7 %collective-permute-start.1 = (bf16[48,1664]{1,0:T(8,128)(2,1)}, bf16[48,1664]{1,0:T(8,128)(2,1)S(1)}, u32[]{:S(2)}, u32[]{:S(2)}) collective-permute-start(bf16[48,1664]{1,0:T(8,128)(2,1)} %get-tuple-element.62), channel_id=1, source_target_pairs={{0,8},{2,10},{4,12},{6,14},{8,16},{10,18},{12,20},{14,22},{16,24},... | collective-permute-start | bytes 479240 | tf_op jit(solution)/shard_map/ppermute | solution.py:718
  21.2 35.4 %copy-start.5 = (bf16[48,1664]{1,0:T(8,128)(2,1)}, bf16[48,1664]{1,0:T(8,128)(2,1)S(1)}, u32[]{:S(2)}) copy-start(bf16[48,1664]{1,0:T(8,128)(2,1)S(1)} %collective-permute-done.5.refs_4_) | copy-start | bytes 479236
  21.2 20.4 %collective-permute-start.11 = (bf16[48,1664]{1,0:T(8,128)(2,1)S(1)}, bf16[48,1664]{1,0:T(8,128)(2,1)S(1)}, u32[]{:S(2)}, u32[]{:S(2)}) collective-permute-start(bf16[48,1664]{1,0:T(8,128)(2,1)S(1)} %collective-permute-done.5.refs_4_), channel_id=1, source_target_pairs={{0,4},{2,6},{4,0},{6,2},{8,12},{10,14},{12,8},{14,10},{16,20},{18,... | collective-permute-start | bytes 479240 | tf_op jit(solution)/shard_map/ppermute | solution.py:718
  22.7 27.7 %collective-permute-start = (bf16[48,3328]{1,0:T(8,128)(2,1)}, bf16[48,3328]{1,0:T(8,128)(2,1)S(1)}, u32[]{:S(2)}, u32[]{:S(2)}) collective-permute-start(bf16[48,3328]{1,0:T(8,128)(2,1)} %get-tuple-element.61.own), channel_id=1, source_target_pairs={{0,4},{2,6},{4,0},{6,2},{8,12},{10,14},{12,8},{14,10},{16,20},{18,... | collective-permute-start | bytes 958472 | tf_op jit(solution)/shard_map/ppermute | solution.py:718
  23.2 18.4 %collective-permute-start.6 = (bf16[48,1664]{1,0:T(8,128)(2,1)S(1)}, bf16[48,1664]{1,0:T(8,128)(2,1)S(1)}, u32[]{:S(2)}, u32[]{:S(2)}) collective-permute-start(bf16[48,1664]{1,0:T(8,128)(2,1)S(1)} %collective-permute-done.5.refs_4_), channel_id=1, source_target_pairs={{0,1},{1,0},{2,3},{3,2},{4,5},{5,4},{6,7},{7,6},{8,9},{9,8},{10,11... | collective-permute-start | bytes 479240 | tf_op jit(solution)/shard_map/ppermute | solution.py:722
  37.8 18.7 %copy-start.6 = (bf16[48,1664]{1,0:T(8,128)(2,1)}, bf16[48,1664]{1,0:T(8,128)(2,1)S(1)}, u32[]{:S(2)}) copy-start(bf16[48,1664]{1,0:T(8,128)(2,1)S(1)} %collective-permute-done.3.refs_2_) | copy-start | bytes 479236
  37.8 6.1 %collective-permute-start.9 = (bf16[48,1664]{1,0:T(8,128)(2,1)S(1)}, bf16[48,1664]{1,0:T(8,128)(2,1)S(1)}, u32[]{:S(2)}, u32[]{:S(2)}) collective-permute-start(bf16[48,1664]{1,0:T(8,128)(2,1)S(1)} %collective-permute-done.3.refs_2_), channel_id=1, source_target_pairs={{0,4},{2,6},{4,0},{6,2},{8,12},{10,14},{12,8},{14,10},{16,20},{18,... | collective-permute-start | bytes 479240 | tf_op jit(solution)/shard_map/ppermute | solution.py:718
  40.0 16.5 %copy-start.7 = (bf16[48,1664]{1,0:T(8,128)(2,1)}, bf16[48,1664]{1,0:T(8,128)(2,1)S(1)}, u32[]{:S(2)}) copy-start(bf16[48,1664]{1,0:T(8,128)(2,1)S(1)} %collective-permute-done.1.refs_0_) | copy-start | bytes 479236
  40.0 7.0 %collective-permute-start.4 = (bf16[48,1664]{1,0:T(8,128)(2,1)S(1)}, bf16[48,1664]{1,0:T(8,128)(2,1)S(1)}, u32[]{:S(2)}, u32[]{:S(2)}) collective-permute-start(bf16[48,1664]{1,0:T(8,128)(2,1)S(1)} %collective-permute-done.3.refs_2_), channel_id=1, source_target_pairs={{0,1},{1,0},{2,3},{3,2},{4,5},{5,4},{6,7},{7,6},{8,9},{9,8},{10,11... | collective-permute-start | bytes 479240 | tf_op jit(solution)/shard_map/ppermute | solution.py:722
  41.5 15.0 %copy-start.8 = (bf16[48,1664]{1,0:T(8,128)(2,1)}, bf16[48,1664]{1,0:T(8,128)(2,1)S(1)}, u32[]{:S(2)}) copy-start(bf16[48,1664]{1,0:T(8,128)(2,1)S(1)} %collective-permute-done.11.refs_10_) | copy-start | bytes 479236
  41.5 7.0 %collective-permute-start.7 = (bf16[48,1664]{1,0:T(8,128)(2,1)S(1)}, bf16[48,1664]{1,0:T(8,128)(2,1)S(1)}, u32[]{:S(2)}, u32[]{:S(2)}) collective-permute-start(bf16[48,1664]{1,0:T(8,128)(2,1)S(1)} %collective-permute-done.1.refs_0_), channel_id=1, source_target_pairs={{0,4},{2,6},{4,0},{6,2},{8,12},{10,14},{12,8},{14,10},{16,20},{18,... | collective-permute-start | bytes 479240 | tf_op jit(solution)/shard_map/ppermute | solution.py:718
  41.6 11.4 %copy-start.9 = (bf16[48,1664]{1,0:T(8,128)(2,1)}, bf16[48,1664]{1,0:T(8,128)(2,1)S(1)}, u32[]{:S(2)}) copy-start(bf16[48,1664]{1,0:T(8,128)(2,1)S(1)} %collective-permute-done.6.refs_5_) | copy-start | bytes 479236
  41.6 8.8 %collective-permute-start.2 = (bf16[48,1664]{1,0:T(8,128)(2,1)S(1)}, bf16[48,1664]{1,0:T(8,128)(2,1)S(1)}, u32[]{:S(2)}, u32[]{:S(2)}) collective-permute-start(bf16[48,1664]{1,0:T(8,128)(2,1)S(1)} %collective-permute-done.1.refs_0_), channel_id=1, source_target_pairs={{0,1},{1,0},{2,3},{3,2},{4,5},{5,4},{6,7},{7,6},{8,9},{9,8},{10,11... | collective-permute-start | bytes 479240 | tf_op jit(solution)/shard_map/ppermute | solution.py:722
  43.9 10.9 %copy-start.10 = (bf16[48,1664]{1,0:T(8,128)(2,1)}, bf16[48,1664]{1,0:T(8,128)(2,1)S(1)}, u32[]{:S(2)}) copy-start(bf16[48,1664]{1,0:T(8,128)(2,1)S(1)} %collective-permute-done.9.refs_8_) | copy-start | bytes 479236
  43.9 9.1 %collective-permute-start.12 = (bf16[48,1664]{1,0:T(8,128)(2,1)S(1)}, bf16[48,1664]{1,0:T(8,128)(2,1)S(1)}, u32[]{:S(2)}, u32[]{:S(2)}) collective-permute-start(bf16[48,1664]{1,0:T(8,128)(2,1)S(1)} %collective-permute-done.11.refs_10_), channel_id=1, source_target_pairs={{0,1},{1,0},{2,3},{3,2},{4,5},{5,4},{6,7},{7,6},{8,9},{9,8},{10,11... | collective-permute-start | bytes 479240 | tf_op jit(solution)/shard_map/ppermute | solution.py:722
  47.0 7.8 %copy-start.11 = (bf16[48,1664]{1,0:T(8,128)(2,1)}, bf16[48,1664]{1,0:T(8,128)(2,1)S(1)}, u32[]{:S(2)}) copy-start(bf16[48,1664]{1,0:T(8,128)(2,1)S(1)} %collective-permute-done.4.refs_3_) | copy-start | bytes 479236
  47.0 7.8 %collective-permute-start.10 = (bf16[48,1664]{1,0:T(8,128)(2,1)S(1)}, bf16[48,1664]{1,0:T(8,128)(2,1)S(1)}, u32[]{:S(2)}, u32[]{:S(2)}) collective-permute-start(bf16[48,1664]{1,0:T(8,128)(2,1)S(1)} %collective-permute-done.9.refs_8_), channel_id=1, source_target_pairs={{0,1},{1,0},{2,3},{3,2},{4,5},{5,4},{6,7},{7,6},{8,9},{9,8},{10,11... | collective-permute-start | bytes 479240 | tf_op jit(solution)/shard_map/ppermute | solution.py:722
  48.5 6.2 %copy-start.12 = (bf16[48,1664]{1,0:T(8,128)(2,1)}, bf16[48,1664]{1,0:T(8,128)(2,1)S(1)}, u32[]{:S(2)}) copy-start(bf16[48,1664]{1,0:T(8,128)(2,1)S(1)} %collective-permute-done.7.refs_6_) | copy-start | bytes 479236
  48.5 8.0 %collective-permute-start.8 = (bf16[48,1664]{1,0:T(8,128)(2,1)S(1)}, bf16[48,1664]{1,0:T(8,128)(2,1)}, u32[]{:S(2)}, u32[]{:S(2)}) collective-permute-start(bf16[48,1664]{1,0:T(8,128)(2,1)S(1)} %collective-permute-done.7.refs_6_), channel_id=1, source_target_pairs={{0,1},{1,0},{2,3},{3,2},{4,5},{5,4},{6,7},{7,6},{8,9},{9,8},{10,11... | collective-permute-start | bytes 479240 | tf_op jit(solution)/shard_map/ppermute | solution.py:722
  50.4 4.4 %copy-start.13 = (bf16[48,1664]{1,0:T(8,128)(2,1)}, bf16[48,1664]{1,0:T(8,128)(2,1)S(1)}, u32[]{:S(2)}) copy-start(bf16[48,1664]{1,0:T(8,128)(2,1)S(1)} %collective-permute-done.2.refs_1_) | copy-start | bytes 479236
  50.4 6.2 %copy-start.3 = (bf16[48,3328]{1,0:T(8,128)(2,1)}, bf16[48,3328]{1,0:T(8,128)(2,1)S(1)}, u32[]{:S(2)}) copy-start(bf16[48,3328]{1,0:T(8,128)(2,1)S(1)} %collective-permute-done.across) | copy-start | bytes 958468
  53.0 1.7 copy-start.14
  54.8 0.7 copy-start.15
  60.1 5.2 %collective-permute-start.13 = (bf16[8,48,3328]{2,1,0:T(8,128)(2,1)}, bf16[8,48,3328]{2,1,0:T(8,128)(2,1)}, u32[]{:S(2)}, u32[]{:S(2)}) collective-permute-start(bf16[8,48,3328]{2,1,0:T(8,128)(2,1)} %assemble.1.mine), channel_id=1, source_target_pairs={{0,2},{2,0},{4,6},{6,4},{8,10},{10,8},{12,14},{14,12},{16,18},{18,... | collective-permute-start | bytes 7667720 | tf_op jit(solution)/shard_map/ppermute | solution.py:718
  201.7 5.2 %collective-permute-start.14 = (bf16[2,4,48,3328]{3,2,1,0:T(8,128)(2,1)}, bf16[2,4,48,3328]{3,2,1,0:T(8,128)(2,1)}, u32[]{:S(2)}, u32[]{:S(2)}) collective-permute-start(bf16[2,4,48,3328]{3,2,1,0:T(8,128)(2,1)} %get-tuple-element.75), channel_id=1, source_target_pairs={{0,2},{2,0},{4,6},{6,4},{8,10},{10,8},{12,14},{14,12},{16,18},{18,... | collective-permute-start | bytes 7667720 | tf_op jit(solution)/shard_map/ppermute | solution.py:718
  211.5 17.9 %collective-permute-start.15 = (bf16[4,48,1024]{2,1,0:T(8,128)(2,1)}, bf16[4,48,1024]{2,1,0:T(8,128)(2,1)}, u32[]{:S(2)}, u32[]{:S(2)}) collective-permute-start(bf16[4,48,1024]{2,1,0:T(8,128)(2,1)} %get-tuple-element.76.tie.old), channel_id=1, source_target_pairs={{0,4},{2,6},{4,0},{6,2},{8,12},{10,14},{12,8},{14,10},{16,20},{18,... | collective-permute-start | bytes 1179656 | tf_op jit(solution)/shard_map/ppermute | solution.py:718
  211.5 22.1 %collective-permute-start.16 = (bf16[2,4,48,1152]{3,2,1,0:T(8,128)(2,1)}, bf16[2,4,48,1152]{3,2,1,0:T(8,128)(2,1)S(1)}, u32[]{:S(2)}, u32[]{:S(2)}) collective-permute-start(bf16[2,4,48,1152]{3,2,1,0:T(8,128)(2,1)} %get-tuple-element.81), channel_id=1, source_target_pairs={{0,1},{1,0},{2,3},{3,2},{4,5},{5,4},{6,7},{7,6},{8,9},{9,8},{10,11... | collective-permute-start | bytes 2654216 | tf_op jit(solution)/shard_map/ppermute | solution.py:792
  233.5 0.9 copy-start
  237.2 16.5 %collective-permute-start.18 = (bf16[4,48,1152]{2,1,0:T(8,128)(2,1)}, bf16[4,48,1152]{2,1,0:T(8,128)(2,1)S(1)}, u32[]{:S(2)}, u32[]{:S(2)}) collective-permute-start(bf16[4,48,1152]{2,1,0:T(8,128)(2,1)} %get-tuple-element.85), channel_id=1, source_target_pairs={{0,4},{2,6},{4,0},{6,2},{8,12},{10,14},{12,8},{14,10},{16,20},{18,... | collective-permute-start | bytes 1327112 | tf_op jit(solution)/shard_map/ppermute | solution.py:718
  238.9 14.1 %collective-permute-start.17 = (bf16[4,48,512]{2,1,0:T(8,128)(2,1)}, bf16[4,48,512]{2,1,0:T(8,128)(2,1)S(1)}, u32[]{:S(2)}, u32[]{:S(2)}) collective-permute-start(bf16[4,48,512]{2,1,0:T(8,128)(2,1)} %get-tuple-element.83.tie), channel_id=1, source_target_pairs={{0,1},{1,0},{2,3},{3,2},{4,5},{5,4},{6,7},{7,6},{8,9},{9,8},{10,11... | collective-permute-start | bytes 589832 | tf_op jit(solution)/shard_map/ppermute | solution.py:795
  253.0 0.7 copy-start.4
  253.7 0.8 copy-start.2
  266.6 19.0 %collective-permute-start.23 = (bf16[48,6144]{1,0:T(8,128)(2,1)}, bf16[48,6144]{1,0:T(8,128)(2,1)S(1)}, u32[]{:S(2)}, u32[]{:S(2)}) collective-permute-start(bf16[48,6144]{1,0:T(8,128)(2,1)} %reduce-scatter.2.cloned.1.call-done.a_ref), channel_id=1, source_target_pairs={{0,1},{1,0},{2,3},{3,2},{4,5},{5,4},{6,7},{7,6},{8,9},{9,8},{10,11... | collective-permute-start | bytes 1769480 | tf_op jit(solution)/shard_map/ppermute | solution.py:801
  268.0 14.4 %collective-permute-start.19 = (bf16[48,1664]{1,0:T(8,128)(2,1)}, bf16[48,1664]{1,0:T(8,128)(2,1)S(1)}, u32[]{:S(2)}, u32[]{:S(2)}) collective-permute-start(bf16[48,1664]{1,0:T(8,128)(2,1)} %get-tuple-element.88), channel_id=1, source_target_pairs={{0,16},{2,18},{4,20},{6,22},{8,24},{10,26},{12,28},{14,30},{16,0},... | collective-permute-start | bytes 479240 | tf_op jit(solution)/shard_map/ppermute | solution.py:718
  270.0 12.4 %collective-permute-start.21 = (bf16[48,1664]{1,0:T(8,128)(2,1)}, bf16[48,1664]{1,0:T(8,128)(2,1)S(1)}, u32[]{:S(2)}, u32[]{:S(2)}) collective-permute-start(bf16[48,1664]{1,0:T(8,128)(2,1)} %get-tuple-element.92.tie), channel_id=1, source_target_pairs={{0,24},{2,26},{4,28},{6,30},{8,0},{10,2},{12,4},{14,6},{16,8},{18,... | collective-permute-start | bytes 479240 | tf_op jit(solution)/shard_map/ppermute | solution.py:718
  271.8 10.6 %collective-permute-start.20 = (bf16[48,1664]{1,0:T(8,128)(2,1)}, bf16[48,1664]{1,0:T(8,128)(2,1)}, u32[]{:S(2)}, u32[]{:S(2)}) collective-permute-start(bf16[48,1664]{1,0:T(8,128)(2,1)} %get-tuple-element.91), channel_id=1, source_target_pairs={{0,8},{2,10},{4,12},{6,14},{8,16},{10,18},{12,20},{14,22},{16,24},... | collective-permute-start | bytes 479240 | tf_op jit(solution)/shard_map/ppermute | solution.py:718
  282.4 0.7 copy-start.16
  282.4 0.7 copy-start.17
  285.0 5.5 %collective-permute-start.22 = (bf16[48,1664]{1,0:T(8,128)(2,1)}, bf16[48,1664]{1,0:T(8,128)(2,1)S(1)}, u32[]{:S(2)}, u32[]{:S(2)}) collective-permute-start(bf16[48,1664]{1,0:T(8,128)(2,1)} %along_sum.1.tie.a_ref), channel_id=1, source_target_pairs={{0,1},{1,0},{2,3},{3,2},{4,5},{5,4},{6,7},{7,6},{8,9},{9,8},{10,11... | collective-permute-start | bytes 479240 | tf_op jit(solution)/shard_map/ppermute | solution.py:804
  285.6 0.8 copy-start.1
  290.5 0.7 copy-start.18
Sparse Core Ops, SparseCore 0:
  10.9 90.8 all-gather.1
  153.8 112.7 reduce-scatter.1
